TPU v7x, 128 devices: a whole 4x4x4 slice. The times are simulated.
128 devices in a mesh: dp: 4 (over x), seq: 32 (over y, z, core).
Axes of the slice: x: 4, y: 4, z: 4, core: 2. Of those that a mesh axis runs over, the one named last changes fastest.
Arguments:
- tokens: bfloat16 [4, 16384, 1024], P('dp', 'seq'), may hold values from -6 to 6
- w_query: bfloat16 [1024, 1024], replicated, may hold values from -0.1875 to 0.1875
- w_key: bfloat16 [1024, 1024], replicated, may hold values from -0.1875 to 0.1875
- w_value: bfloat16 [1024, 1024], replicated, may hold values from -0.1875 to 0.1875
- proj_keys: bfloat16 [256, 16384], P(None, 'seq'), may hold values from -0.1875 to 0.1875
- proj_values: bfloat16 [256, 16384], P(None, 'seq'), may hold values from -0.1875 to 0.1875
- grad_out: bfloat16 [4, 16384, 1024], P('dp', 'seq'), may hold values from -6 to 6
Outputs:
- attended: bfloat16 [4, 16384, 1024], P('dp', 'seq')
- grad_tokens: bfloat16 [4, 16384, 1024], P('dp', 'seq')
- weight_grads: float32 [1024, 3072], P(('dp', 'seq'))
All inputs are finite; a program needn't handle non-finite values.
Results may differ from a plain program's by a relative error of at most 0.013.
The roundings to bfloat16 on the way count: a program that leaves them out, or rounds other values in their place, can miss the bound.
Values sent between devices are 32-bit elements; how exact they have to be, the bound alone decides.
No kernel may reach another device: no remote copies, remote signals or barrier semaphores. Data moves between devices by JAX's collectives and lax.ppermute only.
A program may use at most 128 MiB of HBM per device.

v0:
```python
import jax
import jax.numpy as jnp
from jax import lax
from jax.sharding import PartitionSpec as P

D = 1024
HEADS = 16
HEAD_DIM = 64
PROJ = 256


def exact_einsum(form, left, right):
    return jnp.einsum(
        form, left, right, preferred_element_type=jnp.float32, precision=lax.Precision.HIGHEST
    )


def per_device(tokens, w_query, w_key, w_value, proj_keys, proj_values, grad_out):
    inputs = tokens[0]
    upstream = grad_out[0]
    length = inputs.shape[0]
    key_weight = w_key.astype(jnp.float32)
    value_weight = w_value.astype(jnp.float32)
    query = jnp.dot(inputs, w_query, preferred_element_type=jnp.float32).astype(jnp.bfloat16)
    key_part = jnp.dot(proj_keys, inputs, preferred_element_type=jnp.float32)
    value_part = jnp.dot(proj_values, inputs, preferred_element_type=jnp.float32)
    key_tokens, value_tokens = lax.psum((key_part, value_part), "seq")
    key_proj = exact_einsum("pe,ed->pd", key_tokens, key_weight).astype(jnp.bfloat16)
    value_proj = exact_einsum("pe,ed->pd", value_tokens, value_weight).astype(jnp.bfloat16)
    query_h = query.reshape(length, HEADS, HEAD_DIM)
    key_h = key_proj.reshape(PROJ, HEADS, HEAD_DIM)
    value_h = value_proj.reshape(PROJ, HEADS, HEAD_DIM)
    grad_h = upstream.reshape(length, HEADS, HEAD_DIM)
    scores = jnp.einsum("shd,phd->hsp", query_h, key_h, preferred_element_type=jnp.float32) * 0.125
    probs = jax.nn.softmax(scores, axis=-1)
    probs_low = probs.astype(jnp.bfloat16)
    attended = (
        jnp.einsum("hsp,phd->shd", probs_low, value_h, preferred_element_type=jnp.float32)
        .astype(jnp.bfloat16)
        .reshape(length, D)
    )
    dprobs = jnp.einsum("shd,phd->hsp", grad_h, value_h, preferred_element_type=jnp.float32)
    dscores = (probs * (dprobs - jnp.sum(dprobs * probs, axis=-1, keepdims=True)) * 0.125).astype(
        jnp.bfloat16
    )
    grad_query = (
        jnp.einsum("hsp,phd->shd", dscores, key_h, preferred_element_type=jnp.float32)
        .astype(jnp.bfloat16)
        .reshape(length, D)
    )
    gk_part = jnp.einsum(
        "hsp,shd->phd", dscores, query_h, preferred_element_type=jnp.float32
    ).reshape(PROJ, D)
    gv_part = jnp.einsum(
        "hsp,shd->phd", probs_low, grad_h, preferred_element_type=jnp.float32
    ).reshape(PROJ, D)
    gk_sum, gv_sum = lax.psum((gk_part, gv_part), "seq")
    grad_key_tokens = exact_einsum("pe,de->pd", gk_sum, key_weight).astype(jnp.bfloat16)
    grad_value_tokens = exact_einsum("pe,de->pd", gv_sum, value_weight).astype(jnp.bfloat16)
    grad_tokens = jnp.einsum("se,de->sd", grad_query, w_query, preferred_element_type=jnp.float32)
    grad_tokens = grad_tokens + jnp.einsum(
        "ps,pd->sd", proj_keys, grad_key_tokens, preferred_element_type=jnp.float32
    )
    grad_tokens = grad_tokens + jnp.einsum(
        "ps,pd->sd", proj_values, grad_value_tokens, preferred_element_type=jnp.float32
    )
    grad_tokens = grad_tokens.astype(jnp.bfloat16)
    row_count = D // lax.axis_size(("dp", "seq"))
    seq_size = lax.axis_size("seq")
    seq_place = lax.axis_index("seq")
    share = PROJ // seq_size
    offset = seq_place * share
    key_share = lax.dynamic_slice_in_dim(key_tokens, offset, share, 0)
    value_share = lax.dynamic_slice_in_dim(value_tokens, offset, share, 0)
    gk_share = lax.dynamic_slice_in_dim(gk_sum, offset, share, 0)
    gv_share = lax.dynamic_slice_in_dim(gv_sum, offset, share, 0)
    total = lax.psum(
        jnp.concatenate(
            [
                jnp.einsum("sc,se->ce", inputs, grad_query, preferred_element_type=jnp.float32),
                exact_einsum("pc,pe->ce", key_share, gk_share),
                exact_einsum("pc,pe->ce", value_share, gv_share),
            ],
            axis=1,
        ),
        ("dp", "seq"),
    )
    squared = jnp.sum(total * total)
    mine = lax.dynamic_slice_in_dim(total, lax.axis_index(("dp", "seq")) * row_count, row_count, 0)
    clip = jnp.minimum(1.0, lax.rsqrt(squared + 1e-06))
    return (attended[None], grad_tokens[None], mine * clip)


def solution(mesh):
    return jax.shard_map(
        per_device,
        mesh=mesh,
        in_specs=(
            P("dp", "seq", None),
            P(),
            P(),
            P(),
            P(None, "seq"),
            P(None, "seq"),
            P("dp", "seq", None),
        ),
        out_specs=(P("dp", "seq", None), P("dp", "seq", None), P(("dp", "seq"), None)),
        check_vma=False,
    )
```

profile of v0, /device:TPU:1, one launch (start us, length us, event | category | flops | bytes accessed | tf_op | source)
XLA Modules:
  0.0 483.8 jit_solution(8815172128664737602)
XLA Ops:
  7.2 2.9 fusion.23
  10.1 2.7 fusion.26
  12.9 1.5 copy.30
  14.4 3.5 convolution_convert_fusion
  17.9 2.4 copy.27
  20.3 103.6 %all-reduce.10.cloned.1.call-done = (f32[256,1024]{1,0:T(8,128)}, f32[256,1024]{1,0:T(8,128)}) async-done(((f32[256,1024]{1,0:T(8,128)}, f32[256,1024]{1,0:T(8,128)}), (f32[256,1024]{1,0:T(8,128)}, f32[256,1024]{1,0:T(8,128)})) %all-reduce.10.cloned.1.call-update) | async-done | bytes 2097168 | tf_op jit(solution)/shard_map/psum | solution.py:27
  123.9 4.5 convolution_convert_fusion.4
  128.4 2.0 copy.26
  130.5 4.5 convolution_convert_fusion.3
  135.0 2.0 copy.28
  137.0 5.6 %fusion.44 = f32[16,256,512]{2,1,0:T(8,128)} fusion(bf16[256,16,64]{0,2,1:T(8,128)(2,1)} %bitcast.97, bf16[512,16,64]{0,2,1:T(8,128)(2,1)S(1)} %bitcast.95), kind=kOutput, calls=%fused_computation.55 | convolution fusion | flops 268435456 | bytes 9961472 | tf_op jit(solution)/shard_map/shd,phd->hsp/dot_general | solution.py:42
  142.6 7.4 %fusion.43 = (f32[16,512]{1,0:T(8,128)S(1)}, f32[16,512,256]{1,2,0:T(8,128)}) fusion(bf16[512,16,64]{0,2,1:T(8,128)(2,1)} %bitcast.101, bf16[256,16,64]{0,2,1:T(8,128)(2,1)} %bitcast.104), kind=kOutput, calls=%fused_computation.54 | convolution fusion | flops 274727168 | bytes 9994240 | tf_op jit(solution)/shard_map/sub | solution.py:35
  150.0 5.8 %fusion.13 = f32[16,256,64]{1,2,0:T(8,128)} fusion(bf16[512,16,64]{0,2,1:T(8,128)(2,1)S(1)} %bitcast.96, f32[16,512,256]{1,2,0:T(8,128)} %get-tuple-element.14, f32[16,512]{1,0:T(8,128)S(1)} %get-tuple-element.13), kind=kOutput, calls=%fused_computation.21 | convolution fusion | flops 272629760 | bytes 10518528 | tf_op jit(solution)/shard_map/hsp,shd->phd/dot_general | solution.py:54
  155.7 15.0 %fusion.10 = f32[16,64,256]{2,1,0:T(8,128)} fusion(bf16[512,16,64]{0,2,1:T(8,128)(2,1)} %bitcast.102, f32[16,256,512]{2,1,0:T(8,128)} %fusion.44, f32[16,512,256]{1,2,0:T(8,128)} %get-tuple-element.14, f32[16,512]{1,0:T(8,128)S(1)} %get-tuple-element.13), kind=kOutput, calls=%fused_computation.15 | convolution fusion | flops 283123968 | bytes 18907136 | tf_op jit(solution)/shard_map/hsp,shd->phd/dot_general | solution.py:51
  171.1 15.1 %fusion.20 = bf16[16,64,512]{2,1,0:T(8,128)(2,1)} fusion(bf16[256,16,64]{0,2,1:T(8,128)(2,1)} %bitcast.105, f32[16,256,512]{2,1,0:T(8,128)} %fusion.44, f32[16,512,256]{1,2,0:T(8,128)} %get-tuple-element.14, f32[16,512]{1,0:T(8,128)S(1)} %get-tuple-element.13), kind=kOutput, calls=%fused_computation.27 | convolution fusion | flops 283648256 | bytes 18382848 | tf_op jit(solution)/shard_map/hsp,phd->shd/dot_general | solution.py:47
  186.2 4.4 convolution_bitcast_fusion
  190.6 87.6 %all-reduce.8.cloned.1.call-done = (f32[256,1024]{0,1:T(8,128)}, f32[256,1024]{0,1:T(8,128)}) async-done(((f32[256,1024]{0,1:T(8,128)}, f32[256,1024]{0,1:T(8,128)}), (f32[256,1024]{0,1:T(8,128)}, f32[256,1024]{0,1:T(8,128)})) %all-reduce.8.cloned.1.call-update) | async-done | bytes 2097168 | tf_op jit(solution)/shard_map/psum | solution.py:57
  278.2 4.7 fusion.32
  282.9 4.5 fusion.30
  287.4 5.7 %pad_maximum_fusion = f32[1024,3072]{0,1:T(8,128)} fusion(f32[1024,1024]{0,1:T(8,128)S(1)} %fusion.30, f32[1024,1024]{0,1:T(8,128)S(1)} %fusion.32, f32[1024,1024]{0,1:T(8,128)S(1)} %copy-done.4), kind=kLoop, calls=%fused_computation.2 | loop fusion | flops 6291456 | bytes 25165824 | tf_op jit(solution)/shard_map/concatenate | solution.py:78
  293.1 1.0 copy-done.7
  294.1 5.2 %fusion.17 = bf16[16,64,512]{2,1,0:T(8,128)(2,1)} fusion(bf16[256,16,64]{0,2,1:T(8,128)(2,1)S(1)} %bitcast.98, f32[16,512,256]{1,2,0:T(8,128)} %get-tuple-element.14, f32[16,512]{1,0:T(8,128)S(1)} %get-tuple-element.13), kind=kOutput, calls=%fused_computation.26 | convolution fusion | flops 273154048 | bytes 9994240 | tf_op jit(solution)/shard_map/hsp,phd->shd/dot_general | solution.py:38
  299.4 2.6 copy.36
  302.0 2.7 fusion.45
  304.8 3.5 convolution_convert_fusion.2
  308.3 0.5 fusion.46
  308.8 3.5 convolution_convert_fusion.1
  312.3 1.5 fusion.21
  313.8 148.4 %all-reduce.6.cloned.1.call-done = f32[1024,3072]{0,1:T(8,128)} async-done(((f32[1024,3072]{0,1:T(8,128)}), f32[1024,3072]{0,1:T(8,128)}) %all-reduce.6.cloned.1.call-update) | async-done | bytes 12582928 | tf_op jit(solution)/shard_map/psum | solution.py:77
  462.2 8.4 %multiply_reduce_fusion = f32[]{:T(128)} fusion(f32[1024,3072]{0,1:T(8,128)} %all-reduce.6.cloned.1.call-done), kind=kLoop, calls=%fused_computation.3 | loop fusion | flops 6291455 | bytes 12582916 | tf_op jit(solution)/shard_map/reduce_sum | solution.py:88
  471.3 3.1 dynamic-slice_multiply_fusion
  474.4 2.5 copy.37
  (25 shorter events, 0.4 us)
Async XLA Ops:
  7.2 7.2 %copy-start = (bf16[1024,1024]{1,0:T(8,128)(2,1)S(1)}, bf16[1024,1024]{1,0:T(8,128)(2,1)}, u32[]{:S(2)}) copy-start(bf16[1024,1024]{1,0:T(8,128)(2,1)} %param.8) | copy-start | bytes 6291460
  7.2 116.7 %all-reduce.10.cloned.1.call-start = ((), (), s32[]{:S(2)}) async-start(), calls=%async_computation.2 | async-start | bytes 4194304 | tf_op jit(solution)/shard_map/psum | solution.py:27
  12.8 265.4 %all-reduce.8.cloned.1.call-start = ((), (), s32[]{:S(2)}) async-start(), calls=%async_computation.1 | async-start | bytes 4194304 | tf_op jit(solution)/shard_map/psum | solution.py:57
  170.8 291.4 %all-reduce.6.cloned.1.call-start = ((), (), s32[]{:S(2)}) async-start(), calls=%async_computation | async-start | bytes 25165824 | tf_op jit(solution)/shard_map/psum | solution.py:77
  171.1 15.2 %copy-start.3 = (bf16[1,512,1024]{2,1,0:T(8,128)(2,1)S(1)}, bf16[1,512,1024]{2,1,0:T(8,128)(2,1)}, u32[]{:S(2)}) copy-start(bf16[1,512,1024]{2,1,0:T(8,128)(2,1)} %param.7) | copy-start | bytes 3145732
  278.2 9.2 %copy-start.4 = (f32[1024,1024]{0,1:T(8,128)S(1)}, f32[1024,1024]{0,1:T(8,128)}, u32[]{:S(2)}) copy-start(f32[1024,1024]{0,1:T(8,128)} %convolution_bitcast_fusion) | copy-start | bytes 12582916
  293.1 1.0 copy-start.7
  299.4 5.4 %copy-start.6 = (f32[256,1024]{0,1:T(8,128)S(1)}, f32[256,1024]{0,1:T(8,128)}, u32[]{:S(2)}) copy-start(f32[256,1024]{0,1:T(8,128)} %get-tuple-element.10) | copy-start | bytes 3145732
  299.4 8.9 %copy-start.9 = (bf16[256,512]{1,0:T(8,128)(2,1)S(1)}, bf16[256,512]{1,0:T(8,128)(2,1)}, u32[]{:S(2)}) copy-start(bf16[256,512]{1,0:T(8,128)(2,1)} %param.11) | copy-start | bytes 786436
  302.0 2.8 copy-start.1
  302.0 6.8 %copy-start.2 = (bf16[1024,1024]{1,0:T(8,128)(2,1)S(1)}, bf16[1024,1024]{1,0:T(8,128)(2,1)}, u32[]{:S(2)}) copy-start(bf16[1024,1024]{1,0:T(8,128)(2,1)} %param.10) | copy-start | bytes 6291460
  302.0 6.8 %copy-start.5 = (f32[256,1024]{0,1:T(8,128)S(1)}, f32[256,1024]{0,1:T(8,128)}, u32[]{:S(2)}) copy-start(f32[256,1024]{0,1:T(8,128)} %get-tuple-element.9) | copy-start | bytes 3145732
  302.0 10.3 %copy-start.8 = (bf16[256,512]{1,0:T(8,128)(2,1)S(1)}, bf16[256,512]{1,0:T(8,128)(2,1)}, u32[]{:S(2)}) copy-start(bf16[256,512]{1,0:T(8,128)(2,1)} %param.12) | copy-start | bytes 786436
Sparse Core Ops, SparseCore 0:
  12.9 110.9 all-reduce.9
  170.9 107.2 all-reduce.7
  293.3 168.8 all-reduce.5
where the time goes:
time: 487 us; the launch traced here: 484 us
  waiting for transfers between devices  340 us (70%)
  matrix products  97.5 us (20%)
  other arithmetic  17.2 us (4%)
  between operations  15.1 us (3%)
  local copies, waits for them, and re-layouts  14.1 us (3%)
    psum x1, waiting for transfers between devices, per_device(): lax.psum(jnp.concatenate([jnp.einsum('sc,se->ce', inputs, grad_query, pre...  148 us
    psum x1, waiting for transfers between devices, per_device(): key_tokens, value_tokens = lax.psum((key_part, value_part), 'seq')  104 us
    psum x1, waiting for transfers between devices, per_device(): gk_sum, gv_sum = lax.psum((gk_part, gv_part), 'seq')  87.6 us
    dot_general x6, matrix products, exact_einsum(): jnp.einsum(form, left, right, preferred_element_type=jnp.float32, precisi...  25.3 us
    dot_general x1, matrix products, per_device(): jnp.einsum('hsp,phd->shd', dscores, key_h, preferred_element_type=jnp.flo...  15.1 us
    dot_general x1, matrix products, per_device(): jnp.einsum('hsp,shd->phd', dscores, query_h, preferred_element_type=jnp.f...  15 us
  transfers between devices with their start and end apart: 3, of which 3 were waited for; matrix products, arithmetic and copies ran while one was open for 10% of the time, Pallas kernels for 0%

commit v1 on v0

v1 whole, which is shorter than its diff:
```python
import jax
import jax.numpy as jnp
from jax import lax
from jax.experimental import pallas as pl
from jax.experimental.pallas import tpu as pltpu
from jax.sharding import PartitionSpec as P

D = 1024
HEADS = 16
HEAD_DIM = 64
PROJ = 256
DP = 4
CHIPS = 16
SEQ = "seq"
F32 = jnp.float32
BF16 = jnp.bfloat16
LOG2E = 1.4426950408889634


def place(y, z, core):
    return ((y % 4) * 4 + z % 4) * 2 + core % 2


def moved(dy, dz, dcore):
    return [
        (place(y, z, c), place(y + dy, z + dz, c + dcore))
        for y in range(4)
        for z in range(4)
        for c in range(2)
    ]


SAME_CORE = [[2 * chip + core for chip in range(CHIPS)] for core in range(2)]


def swap_cores(x):
    return lax.ppermute(x, SEQ, moved(0, 0, 1))


def along_x(x, step):
    return lax.ppermute(x, "dp", [(d, (d + step) % DP) for d in range(DP)])


def exchange_chips(x):
    return lax.all_to_all(x, SEQ, 0, 0, axis_index_groups=SAME_CORE)


def scatter_sum(x):
    return jnp.sum(exchange_chips(x.reshape(CHIPS, x.shape[0] // CHIPS, x.shape[1])), axis=0)


def gather_rows(x):
    rows = exchange_chips(jnp.broadcast_to(x[None], (CHIPS, *x.shape)))
    return rows.reshape(CHIPS * x.shape[0], x.shape[1])


def dot_f32(form, left, right, precision=None):
    return jnp.einsum(form, left, right, preferred_element_type=F32, precision=precision)


def mm(left, right, left_dim, right_dim):
    return lax.dot_general(
        left, right, (((left_dim,), (right_dim,)), ((), ())), preferred_element_type=F32
    )


def attention_kernel(query_ref, grad_ref, key_ref, value_ref, att_ref, gq_ref, gk_ref, gv_ref):
    att, gq, gk, gv = [], [], [], []
    for h in range(2):
        rows = pl.ds(h * HEAD_DIM, HEAD_DIM)
        query, grad = query_ref[rows, :], grad_ref[rows, :]
        key, value = key_ref[rows, :].astype(BF16), value_ref[rows, :].astype(BF16)
        scores = mm(key, query, 0, 0)
        top = jnp.max(scores, axis=0, keepdims=True)
        raised = jnp.exp2((scores - top) * (0.125 * LOG2E))
        probs = raised * (1.0 / jnp.sum(raised, axis=0, keepdims=True))
        low = probs.astype(BF16)
        dprobs = mm(value, grad, 0, 0)
        inner = jnp.sum(dprobs * probs, axis=0, keepdims=True)
        dscores = (probs * (dprobs - inner) * 0.125).astype(BF16)
        att.append(mm(value, low, 1, 0))
        gq.append(mm(key, dscores, 1, 0))
        gk.append(mm(dscores, query, 1, 1))
        gv.append(mm(low, grad, 1, 1))
    att_ref[...] = jnp.concatenate(att, axis=0).T.astype(BF16)
    gq_ref[...] = jnp.concatenate(gq, axis=0).T.astype(BF16)
    gk_ref[...] = jnp.concatenate(gk, axis=1)
    gv_ref[...] = jnp.concatenate(gv, axis=1)


def attention(query_t, grad_t, key_t, value_t):
    length = query_t.shape[1]
    wide = pl.BlockSpec((2 * HEAD_DIM, length), lambda i: (i, 0))
    narrow = pl.BlockSpec((2 * HEAD_DIM, PROJ), lambda i: (i, 0))
    return pl.pallas_call(
        attention_kernel,
        grid=(HEADS // 2,),
        in_specs=[wide, wide, narrow, narrow],
        out_specs=[
            pl.BlockSpec((length, 2 * HEAD_DIM), lambda i: (0, i)),
            pl.BlockSpec((length, 2 * HEAD_DIM), lambda i: (0, i)),
            pl.BlockSpec((PROJ, 2 * HEAD_DIM), lambda i: (0, i)),
            pl.BlockSpec((PROJ, 2 * HEAD_DIM), lambda i: (0, i)),
        ],
        out_shape=[
            jax.ShapeDtypeStruct((length, D), BF16),
            jax.ShapeDtypeStruct((length, D), BF16),
            jax.ShapeDtypeStruct((PROJ, D), F32),
            jax.ShapeDtypeStruct((PROJ, D), F32),
        ],
        compiler_params=pltpu.CompilerParams(vmem_limit_bytes=48 * 1024 * 1024),
        cost_estimate=pl.CostEstimate(
            flops=12 * length * PROJ * D, bytes_accessed=8 * 1024 * 1024, transcendentals=length * PROJ * HEADS
        ),
        name="attention",
    )(query_t, grad_t, key_t, value_t)


def grad_tokens_kernel(first_ref, pk_ref, pv_ref, gk_ref, gv_ref, out_ref):
    total = first_ref[...]
    total += mm(pk_ref[...], gk_ref[...].astype(BF16), 0, 0)
    total += mm(pv_ref[...], gv_ref[...].astype(BF16), 0, 0)
    out_ref[...] = total.astype(BF16)


def finish_tokens(first, proj_keys, proj_values, gk_tokens, gv_tokens):
    length = first.shape[0]
    tile = 256
    column = lambda rows: pl.BlockSpec((rows, tile), lambda i: (0, i))
    whole = pl.BlockSpec((PROJ, length), lambda i: (0, 0))
    return pl.pallas_call(
        grad_tokens_kernel,
        grid=(D // tile,),
        in_specs=[column(length), whole, whole, column(PROJ), column(PROJ)],
        out_specs=column(length),
        out_shape=jax.ShapeDtypeStruct((length, D), BF16),
        compiler_params=pltpu.CompilerParams(vmem_limit_bytes=48 * 1024 * 1024),
        cost_estimate=pl.CostEstimate(
            flops=4 * length * PROJ * D, bytes_accessed=6 * 1024 * 1024, transcendentals=0
        ),
        name="grad_tokens",
    )(first, proj_keys, proj_values, gk_tokens, gv_tokens)


def sum_everywhere(x):
    x = x + swap_cores(x)
    x = x + sum(lax.ppermute(x, SEQ, moved(0, k, 0)) for k in (1, 2, 3))
    x = x + sum(lax.ppermute(x, SEQ, moved(k, 0, 0)) for k in (1, 2, 3))
    return x + sum(along_x(x, k) for k in (1, 2, 3))


def per_device(tokens, w_query, w_key, w_value, proj_keys, proj_values, grad_out):
    inputs = tokens[0]
    upstream = grad_out[0]
    seq_place = lax.axis_index(SEQ)
    chip, core = seq_place // 2, seq_place % 2
    dp_place = lax.axis_index("dp")
    first_core = core == 0
    exact = lax.Precision.HIGHEST

    theirs = jnp.where(first_core, proj_values, proj_keys)
    ours = jnp.where(first_core, proj_keys, proj_values)
    my_weight = jnp.where(first_core, w_key, w_value).astype(F32)
    arrived = swap_cores(dot_f32("ps,sd->pd", theirs, inputs))
    part = dot_f32("ps,sd->pd", ours, inputs) + arrived
    my_tokens = gather_rows(scatter_sum(part))
    my_proj_t = dot_f32("pe,ed->dp", my_tokens, my_weight, exact)
    other_proj_t = swap_cores(my_proj_t)
    key_t = jnp.where(first_core, my_proj_t, other_proj_t)
    value_t = jnp.where(first_core, other_proj_t, my_proj_t)

    query_t = dot_f32("sd,de->es", inputs, w_query).astype(BF16)
    attended, grad_query, gk_part, gv_part = attention(query_t, upstream.T, key_t, value_t)

    arrived = swap_cores(jnp.where(first_core, gv_part, gk_part))
    part = jnp.where(first_core, gk_part, gv_part) + arrived
    my_grad = gather_rows(scatter_sum(part))
    my_grad_tokens = dot_f32("pe,de->pd", my_grad, my_weight, exact)
    other_grad_tokens = swap_cores(my_grad_tokens)
    gk_tokens = jnp.where(first_core, my_grad_tokens, other_grad_tokens)
    gv_tokens = jnp.where(first_core, other_grad_tokens, my_grad_tokens)
    direct = dot_f32("se,de->sd", grad_query, w_query)
    grad_tokens = finish_tokens(direct, proj_keys, proj_values, gk_tokens, gv_tokens)

    rows = D // (DP * CHIPS * 2)
    wq = dot_f32("sc,se->ce", inputs, grad_query).reshape(DP, CHIPS, 2, rows, D)
    arrived = swap_cores(lax.dynamic_index_in_dim(wq, 1 - core, 2, keepdims=False))
    wq = lax.dynamic_index_in_dim(wq, core, 2, keepdims=False) + arrived
    at = lambda k: lax.dynamic_index_in_dim(wq, (dp_place + k) % DP, 0, keepdims=False)
    far, half = at(2), CHIPS // 2
    up, down = along_x(far[:half], 1), along_x(far[half:], -1)
    ahead, behind = at(1), at(3)
    ahead = jnp.concatenate([ahead[:half] + up, ahead[half:]], axis=0)
    behind = jnp.concatenate([behind[:half], behind[half:] + down], axis=0)
    wq = at(0) + along_x(ahead, 1) + along_x(behind, -1)
    wq = jnp.sum(exchange_chips(wq), axis=0)

    columns = lax.dynamic_index_in_dim(my_tokens.reshape(PROJ, DP, CHIPS, 2 * rows), chip, 2, keepdims=False)
    wkv = dot_f32("pdr,pe->dre", columns, my_grad, exact)
    quarter = lambda k: lax.dynamic_index_in_dim(wkv, (dp_place + k) % DP, 0, keepdims=False)
    wkv = quarter(0) + along_x(quarter(1), 1) + along_x(quarter(2), 2) + along_x(quarter(3), 3)
    wkv = wkv.reshape(2, rows, D)
    arrived = swap_cores(lax.dynamic_index_in_dim(wkv, 1 - core, 0, keepdims=False))
    mine = lax.dynamic_index_in_dim(wkv, core, 0, keepdims=False)
    wk = jnp.where(first_core, mine, arrived)
    wv = jnp.where(first_core, arrived, mine)
    grads = jnp.concatenate([wq, wk, wv], axis=1)
    squared = sum_everywhere(jnp.full((8, 128), jnp.sum(grads * grads)))[0, 0]
    clip = jnp.minimum(1.0, lax.rsqrt(squared + 1e-06))
    return (attended[None], grad_tokens[None], grads * clip)


def solution(mesh):
    return jax.shard_map(
        per_device,
        mesh=mesh,
        in_specs=(
            P("dp", "seq", None),
            P(),
            P(),
            P(),
            P(None, "seq"),
            P(None, "seq"),
            P("dp", "seq", None),
        ),
        out_specs=(P("dp", "seq", None), P("dp", "seq", None), P(("dp", "seq"), None)),
        check_vma=False,
    )
```

time: 487 us -> 198 us (0.41)
  waiting for transfers between devices: 340 us -> 31.7 us
  matrix products: 97.5 us -> 18.7 us
  starting transfers between devices: 0.33 us -> 49.2 us
  blocking collectives: 0 us -> 42.2 us
  Pallas kernels: 0 us -> 16.8 us
  between operations: 15.1 us -> 1.72 us
    psum x3 -> x0, waiting for transfers between devices: 340 us -> none  [the longest x1 148 us: per_device(): lax.psum(jnp.concatenate([jnp.einsum('sc,se->ce', inputs, grad_query, pre...]
    dot_general x18 -> x8, matrix products: 90.1 us -> 18.7 us  [dot_f32(): jnp.einsum(form, left, right, preferred_element_type=F32, precision=preci...]
    all_to_all x0 -> x2, blocking collectives: none -> 42.2 us  [exchange_chips(): return lax.all_to_all(x, SEQ, 0, 0, axis_index_groups=SAME_CORE)]
    ppermute x0 -> x23, starting transfers between devices: none -> 33.7 us  [the longest x7 17.3 us: swap_cores(): return lax.ppermute(x, SEQ, moved(0, 0, 1))]
    all_to_all x0 -> x3, waiting for transfers between devices: none -> 17.6 us  [exchange_chips(): return lax.all_to_all(x, SEQ, 0, 0, axis_index_groups=SAME_CORE)]
    pallas_call x0 -> x2, Pallas kernels: none -> 16.8 us  [the longest x1 14.1 us: attention(): pl.pallas_call(attention_kernel, grid=(HEADS // 2,), in_specs=[wide, wide...]
    all_to_all x0 -> x3, starting transfers between devices: none -> 15.5 us  [exchange_chips(): return lax.all_to_all(x, SEQ, 0, 0, axis_index_groups=SAME_CORE)]
    ppermute x0 -> x23, waiting for transfers between devices: none -> 14.1 us  [the longest x10 6.47 us: along_x(): return lax.ppermute(x, 'dp', [(d, (d + step) % DP) for d in range(DP)])]
  transfers between devices with their start and end apart: 3 -> 26, of which waited for: 3 -> 10; matrix products, arithmetic and copies ran while one was open for 10% -> 19% of each run, Pallas kernels for 0% -> 0%
where the time goes in v1:
time: 198 us; the launch traced here: 197 us
  starting transfers between devices  49.2 us (25%)
  blocking collectives  42.2 us (21%)
  waiting for transfers between devices  31.7 us (16%)
  local copies, waits for them, and re-layouts  18.9 us (10%)
  matrix products  18.7 us (9%)
  other arithmetic  17.3 us (9%)
  Pallas kernels  16.8 us (8%)
    all_to_all x2, blocking collectives, exchange_chips(): return lax.all_to_all(x, SEQ, 0, 0, axis_index_groups=SAME_CORE)  42.2 us
    dot_general x8, matrix products, dot_f32(): jnp.einsum(form, left, right, preferred_element_type=F32, precision=preci...  18.7 us
    all_to_all x3, waiting for transfers between devices, exchange_chips(): return lax.all_to_all(x, SEQ, 0, 0, axis_index_groups=SAME_CORE)  17.6 us
    ppermute x7, starting transfers between devices, swap_cores(): return lax.ppermute(x, SEQ, moved(0, 0, 1))  17.3 us
    all_to_all x3, starting transfers between devices, exchange_chips(): return lax.all_to_all(x, SEQ, 0, 0, axis_index_groups=SAME_CORE)  15.5 us
    pallas_call x1, Pallas kernels, attention(): pl.pallas_call(attention_kernel, grid=(HEADS // 2,), in_specs=[wide, wide...  14.1 us
    ppermute x10, starting transfers between devices, along_x(): return lax.ppermute(x, 'dp', [(d, (d + step) % DP) for d in range(DP)])  12.4 us
    ppermute x10, waiting for transfers between devices, along_x(): return lax.ppermute(x, 'dp', [(d, (d + step) % DP) for d in range(DP)])  6.47 us
  transfers between devices with their start and end apart: 26, of which 10 were waited for; matrix products, arithmetic and copies ran while one was open for 19% of the time, Pallas kernels for 0%

profile of v1, /device:TPU:1, one launch (start us, length us, event | category | flops | bytes accessed | tf_op | source)
XLA Modules:
  0.0 196.6 jit_solution(14502188440263353594)
XLA Ops:
  0.7 1.9 fusion.2
  4.1 2.3 %collective-permute-done = f32[256,1024]{1,0:T(8,128)S(1)} collective-permute-done((f32[256,1024]{1,0:T(8,128)S(1)}, f32[256,1024]{1,0:T(8,128)S(1)}, u32[]{:S(2)}, u32[]{:S(2)}) %collective-permute-start) | collective-permute-done | bytes 1048608 | tf_op jit(solution)/shard_map/ppermute | solution.py:37
  6.8 23.7 %all_to_all.25 = f32[16,16,1024]{2,1,0:T(8,128)} all-to-all(f32[16,16,1024]{2,1,0:T(8,128)S(1)} %bitcast.84), channel_id=1, replica_groups={{0,2,4,6,8,10,12,14,16,18,20,22,24,26,28,30},{1,3,5,7,9,11,13,15,17,19,..., dimensions={0} | all-to-all | bytes 2097152 | tf_op jit(solution)/shard_map/all_to_all | solution.py:45
  32.0 18.5 %all_to_all.26 = f32[16,16,1024]{2,1,0:T(8,128)S(1)} all-to-all(f32[16,16,1024]{2,1,0:T(8,128)S(1)} %broadcast_in_dim.10), channel_id=1, replica_groups={{0,2,4,6,8,10,12,14,16,18,20,22,24,26,28,30},{1,3,5,7,9,11,13,15,17,19,..., dimensions={0} | all-to-all | bytes 2097152 | tf_op jit(solution)/shard_map/all_to_all | solution.py:45
  50.5 5.4 %fusion.7 = f32[1024,256]{1,0:T(8,128)} fusion(f32[256,1024]{1,0:T(8,128)S(1)} %bitcast.82, bf16[1024,1024]{1,0:T(8,128)(2,1)S(1)} %copy-done.10, bf16[1024,1024]{1,0:T(8,128)(2,1)} %param.10, pred[]{:T(512)S(6)} %eq.13), kind=kOutput, calls=%fused_computation.13 | convolution fusion | flops 3222274048 | bytes 6291457 | tf_op jit(solution)/shard_map/pe,ed->dp/dot_general | solution.py:58
  57.2 2.3 %copy.11 = bf16[1,512,1024]{1,2,0:T(8,128)(2,1)} copy(bf16[1,512,1024]{2,1,0:T(8,128)(2,1)} %param.13) | data formatting | bytes 2097152 | tf_op args[6]
  59.4 2.5 %convolution_convert_fusion.query_ref = bf16[1024,512]{1,0:T(8,128)(2,1)S(1)} fusion(bf16[1024,1024]{1,0:T(8,128)(2,1)S(1)} %copy-done, bf16[1,512,1024]{2,1,0:T(8,128)(2,1)} %param.7), kind=kOutput, calls=%fused_computation.3 | convolution fusion | flops 1074266112 | bytes 4194304 | tf_op jit(solution)/shard_map/sd,de->es/dot_general | solution.py:58
  62.0 3.1 %broadcast_select_fusion.6 = (f32[1024,256]{1,0:T(8,128)}, f32[1024,256]{1,0:T(8,128)}) fusion(f32[1024,256]{1,0:T(8,128)} %collective-permute-done.1, f32[1024,256]{1,0:T(8,128)} %fusion.7, pred[]{:T(512)S(6)} %eq.13), kind=kLoop, calls=%fused_computation.21 | loop fusion | flops 524288 | bytes 4194305 | tf_op jit(solution)/shard_map/jit(_where)/select_n | solution.py:170
  65.0 14.1 %attention.1 = (bf16[512,1024]{1,0:T(8,128)(2,1)}, bf16[512,1024]{1,0:T(8,128)(2,1)S(1)}, f32[256,1024]{1,0:T(8,128)S(1)}, f32[256,1024]{1,0:T(8,128)S(1)}) custom-call(bf16[1024,512]{1,0:T(8,128)(2,1)S(1)} %convolution_convert_fusion.query_ref, bf16[1024,512]{1,0:T(8,128)(2,1)S(1)} %bitcast.79, f32[1024,256]{1,0:T(8,128)} %get-tuple-element.20.key_ref, ...), custom_call_target="tpu_custom_call" | custom-call | flops 1610612736 | bytes 8388608 | tf_op jit(solution)/shard_map/attention/pallas_call | solution.py:95
  82.1 1.6 dynamic-slice_bitcast_fusion
  86.0 4.3 %all-to-all-start.2 = ((f32[16,16,1024]{2,1,0:T(8,128)}), f32[16,16,1024]{2,1,0:T(8,128)}, u32[]{:S(2)}, u32[]{:S(2)}) async-start(f32[16,16,1024]{2,1,0:T(8,128)} %bitcast.83), calls=%async_computation.2 | async-start | bytes 2097152 | tf_op jit(solution)/shard_map/all_to_all | solution.py:45
  90.4 15.8 %all-to-all-done.2 = f32[16,16,1024]{2,1,0:T(8,128)} async-done(((f32[16,16,1024]{2,1,0:T(8,128)}), f32[16,16,1024]{2,1,0:T(8,128)}, u32[]{:S(2)}, u32[]{:S(2)}) %all-to-all-start.2) | async-done | bytes 1048608 | tf_op jit(solution)/shard_map/all_to_all | solution.py:45
  108.6 4.5 %all-to-all-start.3 = ((f32[16,16,1024]{2,1,0:T(8,128)}), f32[16,16,1024]{2,1,0:T(8,128)}, u32[]{:S(2)}, u32[]{:S(2)}) async-start(f32[16,16,1024]{2,1,0:T(8,128)} %broadcast_in_dim.23), calls=%async_computation.3 | async-start | bytes 2097152 | tf_op jit(solution)/shard_map/all_to_all | solution.py:45
  113.2 2.6 %bitcast_add_fusion = f32[4,16,8,1024]{3,2,1,0:T(8,128)S(1)} fusion(f32[4,16,8,1024]{3,2,1,0:T(8,128)} %collective-permute-done.4, f32[4,16,2,8,1024]{4,3,2,1,0:T(8,128)} %bitcast.81, s32[]{:T(128)S(6)} %select_n.145), kind=kLoop, calls=%fused_computation | loop fusion | flops 524288 | bytes 6291460 | tf_op jit(solution)/shard_map/add | solution.py:188
  118.7 4.1 %collective-permute-done.5 = f32[8,8,1024]{2,1,0:T(8,128)S(1)} collective-permute-done((f32[8,8,1024]{2,1,0:T(8,128)S(1)}, f32[8,8,1024]{2,1,0:T(8,128)S(1)}, u32[]{:S(2)}, u32[]{:S(2)}) %collective-permute-start.5) | collective-permute-done | bytes 262176 | tf_op jit(solution)/shard_map/ppermute | solution.py:41
  123.8 2.7 %collective-permute-start.8 = (f32[16,8,1024]{2,1,0:T(8,128)}, f32[16,8,1024]{2,1,0:T(8,128)}, u32[]{:S(2)}, u32[]{:S(2)}) collective-permute-start(f32[16,8,1024]{2,1,0:T(8,128)} %pad_maximum_fusion.1), channel_id=1, source_target_pairs={{0,96},{32,0},{64,32},{96,64},{1,97},{33,1},{65,33},{97,65},{2,98}... | collective-permute-start | bytes 1572872 | tf_op jit(solution)/shard_map/ppermute | solution.py:41
  127.4 6.2 %reshape_reshape.3 = f32[256,4,16,16]{3,2,1,0:T(8,128)} reshape(f32[16,16,1024]{2,1,0:T(8,128)} %copy-done.7) | data formatting | bytes 2097152 | tf_op jit(solution)/shard_map/reshape;reshape | solution.py:198
  133.6 2.7 %constant_dynamic-slice_fusion = f32[256,4,1,16]{3,2,1,0:T(1,128)S(1)} fusion(f32[256,4,16,16]{3,2,1,0:T(8,128)} %reshape_reshape.3, s32[]{:T(128)S(6)} %select_n.157), kind=kLoop, calls=%fused_computation.53 | loop fusion | bytes 131076 | tf_op jit(solution)/shard_map/jit(dynamic_index_in_dim)/dynamic_slice | solution.py:198
  136.7 2.0 %fusion.19 = f32[4,16,1024]{2,1,0:T(8,128)S(1)} fusion(f32[256,1024,1]{1,0,2:T(8,128)} %bitcast.22, f32[256,4,1,16]{0,3,1,2:T(8,128)S(1)} %copy.12), kind=kOutput, calls=%fused_computation.42 | convolution fusion | flops 201326592 | bytes 1376256 | tf_op jit(solution)/shard_map/pdr,pe->dre/dot_general | solution.py:58
  139.4 2.7 %collective-permute-start.11 = (f32[16,1024]{1,0:T(8,128)}, f32[16,1024]{1,0:T(8,128)S(1)}, u32[]{:S(2)}, u32[]{:S(2)}) collective-permute-start(f32[16,1024]{1,0:T(8,128)} %get-tuple-element.22), channel_id=1, source_target_pairs={{0,96},{32,0},{64,32},{96,64},{1,97},{33,1},{65,33},{97,65},{2,98}... | collective-permute-start | bytes 196616 | tf_op jit(solution)/shard_map/ppermute | solution.py:41
  143.2 2.2 %fusion.8 = f32[16,8,1024]{2,1,0:T(8,128)} fusion(f32[16,8,1024]{2,1,0:T(8,128)} %collective-permute-done.8, f32[16,8,1024]{2,1,0:T(8,128)} %collective-permute-done.6, f32[4,16,8,1024]{3,2,1,0:T(8,128)} %copy-done.11, s32[]{:T(128)S(6)} %select_n.148), kind=kLoop, calls=%fused_computation.17 | loop fusion | flops 262144 | bytes 2097156 | tf_op jit(solution)/shard_map/add | solution.py:195
  145.5 6.6 %all-to-all-start.4 = ((f32[16,8,1024]{2,1,0:T(8,128)}), f32[16,8,1024]{2,1,0:T(8,128)S(1)}, u32[]{:S(2)}, u32[]{:S(2)}) async-start(f32[16,8,1024]{2,1,0:T(8,128)} %fusion.8), calls=%async_computation.4 | async-start | bytes 1048576 | tf_op jit(solution)/shard_map/all_to_all | solution.py:45
  153.0 5.3 %collective-permute-start.12 = (f32[8,1024]{1,0:T(8,128)S(1)}, f32[8,1024]{1,0:T(8,128)S(1)}, u32[]{:S(2)}, u32[]{:S(2)}) collective-permute-start(f32[8,1024]{1,0:T(8,128)S(1)} %dynamic-slice_bitcast_fusion.10), channel_id=1, source_target_pairs={{0,1},{1,0},{2,3},{3,2},{4,5},{5,4},{6,7},{7,6},{8,9},{9,8},{10,11... | collective-permute-start | bytes 98312 | tf_op jit(solution)/shard_map/ppermute | solution.py:37
  159.2 1.8 all-to-all-done.4
  162.4 6.5 %collective-permute-start.13 = (f32[8,128]{1,0:T(8,128)S(1)}, f32[8,128]{1,0:T(8,128)S(1)}, u32[]{:S(2)}, u32[]{:S(2)}) collective-permute-start(f32[8,128]{1,0:T(8,128)S(1)} %broadcast_in_dim.25), channel_id=1, source_target_pairs={{0,1},{1,0},{2,3},{3,2},{4,5},{5,4},{6,7},{7,6},{8,9},{9,8},{10,11... | collective-permute-start | bytes 12296 | tf_op jit(solution)/shard_map/ppermute | solution.py:37
  170.7 1.8 collective-permute-start.15
  172.8 1.8 collective-permute-done.15
  178.6 3.9 %fusion.6 = f32[256,1024]{1,0:T(8,128)S(1)} fusion(f32[256,1024]{1,0:T(8,128)} %bitcast.7, bf16[1024,1024]{1,0:T(8,128)(2,1)} %param.9, bf16[1024,1024]{1,0:T(8,128)(2,1)} %param.10, pred[]{:T(512)S(6)} %eq.13), kind=kOutput, calls=%fused_computation.12 | convolution fusion | flops 3222274048 | bytes 6291457 | tf_op jit(solution)/shard_map/pe,de->pd/dot_general | solution.py:58
  182.5 2.7 %collective-permute-start.3 = (f32[256,1024]{1,0:T(8,128)S(1)}, f32[256,1024]{1,0:T(8,128)S(1)}, u32[]{:S(2)}, u32[]{:S(2)}) collective-permute-start(f32[256,1024]{1,0:T(8,128)S(1)} %fusion.6), channel_id=1, source_target_pairs={{0,1},{1,0},{2,3},{3,2},{4,5},{5,4},{6,7},{7,6},{8,9},{9,8},{10,11... | collective-permute-start | bytes 3145736 | tf_op jit(solution)/shard_map/ppermute | solution.py:37
  185.5 2.6 %collective-permute-start.21 = (f32[8,128]{1,0:T(8,128)S(1)}, f32[8,128]{1,0:T(8,128)S(1)}, u32[]{:S(2)}, u32[]{:S(2)}) collective-permute-start(f32[8,128]{1,0:T(8,128)S(1)} %add_add_fusion.1), channel_id=1, source_target_pairs={{0,64},{32,96},{64,0},{96,32},{1,65},{33,97},{65,1},{97,33},{2,66}... | collective-permute-start | bytes 12296 | tf_op jit(solution)/shard_map/ppermute | solution.py:41
  189.5 2.3 %collective-permute-done.20 = f32[8,128]{1,0:T(8,128)S(1)} collective-permute-done((f32[8,128]{1,0:T(8,128)S(1)}, f32[8,128]{1,0:T(8,128)S(1)}, u32[]{:S(2)}, u32[]{:S(2)}) %collective-permute-start.20) | collective-permute-done | bytes 4128 | tf_op jit(solution)/shard_map/ppermute | solution.py:41
  193.9 2.7 %grad_tokens.1 = bf16[512,1024]{1,0:T(8,128)(2,1)} custom-call(f32[512,1024]{1,0:T(8,128)S(1)} %fusion.21.first_ref, bf16[256,512]{1,0:T(8,128)(2,1)S(1)} %copy-done.2, bf16[256,512]{1,0:T(8,128)(2,1)S(1)} %copy-done.1, f32[256,1024]{1,0:T(8,128)S(1)} %get-tuple-element.18.gk_ref, f32[256,1024]{1,0:T(8,128)S(1)} %get-tuple-element.17.gv_ref), custom_call_target="tpu_custom_call" | custom-call | flops 536870912 | bytes 6291456 | tf_op jit(solution)/shard_map/grad_tokens/pallas_call | solution.py:131
  (88 shorter events, 31.5 us)
Async XLA Ops:
  0.6 58.8 %copy-start = (bf16[1024,1024]{1,0:T(8,128)(2,1)S(1)}, bf16[1024,1024]{1,0:T(8,128)(2,1)}, u32[]{:S(2)}) copy-start(bf16[1024,1024]{1,0:T(8,128)(2,1)} %param.8) | copy-start | bytes 6291460
  0.6 5.7 %copy-start.1 = (bf16[256,512]{1,0:T(8,128)(2,1)S(1)}, bf16[256,512]{1,0:T(8,128)(2,1)}, u32[]{:S(2)}) copy-start(bf16[256,512]{1,0:T(8,128)(2,1)} %pv_ref.1) | copy-start | bytes 786436
  0.7 5.7 %copy-start.2 = (bf16[256,512]{1,0:T(8,128)(2,1)S(1)}, bf16[256,512]{1,0:T(8,128)(2,1)}, u32[]{:S(2)}) copy-start(bf16[256,512]{1,0:T(8,128)(2,1)} %pk_ref.1) | copy-start | bytes 786436
  2.6 3.8 %collective-permute-start = (f32[256,1024]{1,0:T(8,128)S(1)}, f32[256,1024]{1,0:T(8,128)S(1)}, u32[]{:S(2)}, u32[]{:S(2)}) collective-permute-start(f32[256,1024]{1,0:T(8,128)S(1)} %fusion.2), channel_id=1, source_target_pairs={{0,1},{1,0},{2,3},{3,2},{4,5},{5,4},{6,7},{7,6},{8,9},{9,8},{10,11... | collective-permute-start | bytes 3145736 | tf_op jit(solution)/shard_map/ppermute | solution.py:37
  31.9 18.6 %copy-start.10 = (bf16[1024,1024]{1,0:T(8,128)(2,1)S(1)}, bf16[1024,1024]{1,0:T(8,128)(2,1)}, u32[]{:S(2)}) copy-start(bf16[1024,1024]{1,0:T(8,128)(2,1)} %param.9) | copy-start | bytes 6291460
  55.9 6.1 %collective-permute-start.1 = (f32[1024,256]{1,0:T(8,128)}, f32[1024,256]{1,0:T(8,128)}, u32[]{:S(2)}, u32[]{:S(2)}) collective-permute-start(f32[1024,256]{1,0:T(8,128)} %fusion.7), channel_id=1, source_target_pairs={{0,1},{1,0},{2,3},{3,2},{4,5},{5,4},{6,7},{7,6},{8,9},{9,8},{10,11... | collective-permute-start | bytes 3145736 | tf_op jit(solution)/shard_map/ppermute | solution.py:37
  79.2 5.5 %collective-permute-start.2 = (f32[256,1024]{1,0:T(8,128)S(1)}, f32[256,1024]{1,0:T(8,128)S(1)}, u32[]{:S(2)}, u32[]{:S(2)}) collective-permute-start(f32[256,1024]{1,0:T(8,128)S(1)} %broadcast_select_fusion.5), channel_id=1, source_target_pairs={{0,1},{1,0},{2,3},{3,2},{4,5},{5,4},{6,7},{7,6},{8,9},{9,8},{10,11... | collective-permute-start | bytes 3145736 | tf_op jit(solution)/shard_map/ppermute | solution.py:37
  84.8 28.4 %collective-permute-start.4 = (f32[4,16,8,1024]{3,2,1,0:T(8,128)}, f32[4,16,8,1024]{3,2,1,0:T(8,128)}, u32[]{:S(2)}, u32[]{:S(2)}) collective-permute-start(f32[4,16,8,1024]{3,2,1,0:T(8,128)} %dynamic-slice_bitcast_fusion), channel_id=1, source_target_pairs={{0,1},{1,0},{2,3},{3,2},{4,5},{5,4},{6,7},{7,6},{8,9},{9,8},{10,11... | collective-permute-start | bytes 6291464 | tf_op jit(solution)/shard_map/ppermute | solution.py:37
  86.0 20.2 %all-to-all-start.2 = ((f32[16,16,1024]{2,1,0:T(8,128)}), f32[16,16,1024]{2,1,0:T(8,128)}, u32[]{:S(2)}, u32[]{:S(2)}) async-start(f32[16,16,1024]{2,1,0:T(8,128)} %bitcast.83), calls=%async_computation.2 | async-start | bytes 2097152 | tf_op jit(solution)/shard_map/all_to_all | solution.py:45
  108.6 28.1 %all-to-all-start.3 = ((f32[16,16,1024]{2,1,0:T(8,128)}), f32[16,16,1024]{2,1,0:T(8,128)}, u32[]{:S(2)}, u32[]{:S(2)}) async-start(f32[16,16,1024]{2,1,0:T(8,128)} %broadcast_in_dim.23), calls=%async_computation.3 | async-start | bytes 2097152 | tf_op jit(solution)/shard_map/all_to_all | solution.py:45
  115.8 7.9 %copy-start.11 = (f32[4,16,8,1024]{3,2,1,0:T(8,128)}, f32[4,16,8,1024]{3,2,1,0:T(8,128)S(1)}, u32[]{:S(2)}) copy-start(f32[4,16,8,1024]{3,2,1,0:T(8,128)S(1)} %bitcast_add_fusion) | copy-start | bytes 6291460
  115.9 6.9 %collective-permute-start.5 = (f32[8,8,1024]{2,1,0:T(8,128)S(1)}, f32[8,8,1024]{2,1,0:T(8,128)S(1)}, u32[]{:S(2)}, u32[]{:S(2)}) collective-permute-start(f32[8,8,1024]{2,1,0:T(8,128)S(1)} %get-tuple-element.13), channel_id=1, source_target_pairs={{0,32},{32,64},{64,96},{96,0},{1,33},{33,65},{65,97},{97,1},{2,34}... | collective-permute-start | bytes 786440 | tf_op jit(solution)/shard_map/ppermute | solution.py:41
  117.2 5.6 %collective-permute-start.7 = (f32[8,8,1024]{2,1,0:T(8,128)S(1)}, f32[8,8,1024]{2,1,0:T(8,128)S(1)}, u32[]{:S(2)}, u32[]{:S(2)}) collective-permute-start(f32[8,8,1024]{2,1,0:T(8,128)S(1)} %get-tuple-element.15), channel_id=1, source_target_pairs={{0,96},{32,0},{64,32},{96,64},{1,97},{33,1},{65,33},{97,65},{2,98}... | collective-permute-start | bytes 786440 | tf_op jit(solution)/shard_map/ppermute | solution.py:41
  123.8 19.5 %collective-permute-start.8 = (f32[16,8,1024]{2,1,0:T(8,128)}, f32[16,8,1024]{2,1,0:T(8,128)}, u32[]{:S(2)}, u32[]{:S(2)}) collective-permute-start(f32[16,8,1024]{2,1,0:T(8,128)} %pad_maximum_fusion.1), channel_id=1, source_target_pairs={{0,96},{32,0},{64,32},{96,64},{1,97},{33,1},{65,33},{97,65},{2,98}... | collective-permute-start | bytes 1572872 | tf_op jit(solution)/shard_map/ppermute | solution.py:41
  127.4 15.9 %collective-permute-start.6 = (f32[16,8,1024]{2,1,0:T(8,128)}, f32[16,8,1024]{2,1,0:T(8,128)}, u32[]{:S(2)}, u32[]{:S(2)}) collective-permute-start(f32[16,8,1024]{2,1,0:T(8,128)} %pad_maximum_fusion), channel_id=1, source_target_pairs={{0,32},{32,64},{64,96},{96,0},{1,33},{33,65},{65,97},{97,1},{2,34}... | collective-permute-start | bytes 1572872 | tf_op jit(solution)/shard_map/ppermute | solution.py:41
  139.4 12.7 %collective-permute-start.9 = (f32[16,1024]{1,0:T(8,128)}, f32[16,1024]{1,0:T(8,128)S(1)}, u32[]{:S(2)}, u32[]{:S(2)}) collective-permute-start(f32[16,1024]{1,0:T(8,128)} %get-tuple-element.21), channel_id=1, source_target_pairs={{0,32},{32,64},{64,96},{96,0},{1,33},{33,65},{65,97},{97,1},{2,34}... | collective-permute-start | bytes 196616 | tf_op jit(solution)/shard_map/ppermute | solution.py:41
  139.4 12.7 %collective-permute-start.11 = (f32[16,1024]{1,0:T(8,128)}, f32[16,1024]{1,0:T(8,128)S(1)}, u32[]{:S(2)}, u32[]{:S(2)}) collective-permute-start(f32[16,1024]{1,0:T(8,128)} %get-tuple-element.22), channel_id=1, source_target_pairs={{0,96},{32,0},{64,32},{96,64},{1,97},{33,1},{65,33},{97,65},{2,98}... | collective-permute-start | bytes 196616 | tf_op jit(solution)/shard_map/ppermute | solution.py:41
  142.0 10.1 %collective-permute-start.10 = (f32[16,1024]{1,0:T(8,128)}, f32[16,1024]{1,0:T(8,128)}, u32[]{:S(2)}, u32[]{:S(2)}) collective-permute-start(f32[16,1024]{1,0:T(8,128)} %get-tuple-element.23), channel_id=1, source_target_pairs={{0,64},{32,96},{64,0},{96,32},{1,65},{33,97},{65,1},{97,33},{2,66}... | collective-permute-start | bytes 196616 | tf_op jit(solution)/shard_map/ppermute | solution.py:41
  145.5 15.6 %all-to-all-start.4 = ((f32[16,8,1024]{2,1,0:T(8,128)}), f32[16,8,1024]{2,1,0:T(8,128)S(1)}, u32[]{:S(2)}, u32[]{:S(2)}) async-start(f32[16,8,1024]{2,1,0:T(8,128)} %fusion.8), calls=%async_computation.4 | async-start | bytes 1048576 | tf_op jit(solution)/shard_map/all_to_all | solution.py:45
  153.0 6.2 %collective-permute-start.12 = (f32[8,1024]{1,0:T(8,128)S(1)}, f32[8,1024]{1,0:T(8,128)S(1)}, u32[]{:S(2)}, u32[]{:S(2)}) collective-permute-start(f32[8,1024]{1,0:T(8,128)S(1)} %dynamic-slice_bitcast_fusion.10), channel_id=1, source_target_pairs={{0,1},{1,0},{2,3},{3,2},{4,5},{5,4},{6,7},{7,6},{8,9},{9,8},{10,11... | collective-permute-start | bytes 98312 | tf_op jit(solution)/shard_map/ppermute | solution.py:37
  162.4 7.3 %collective-permute-start.13 = (f32[8,128]{1,0:T(8,128)S(1)}, f32[8,128]{1,0:T(8,128)S(1)}, u32[]{:S(2)}, u32[]{:S(2)}) collective-permute-start(f32[8,128]{1,0:T(8,128)S(1)} %broadcast_in_dim.25), channel_id=1, source_target_pairs={{0,1},{1,0},{2,3},{3,2},{4,5},{5,4},{6,7},{7,6},{8,9},{9,8},{10,11... | collective-permute-start | bytes 12296 | tf_op jit(solution)/shard_map/ppermute | solution.py:37
  170.3 2.5 %collective-permute-start.16 = (f32[8,128]{1,0:T(8,128)S(1)}, f32[8,128]{1,0:T(8,128)S(1)}, u32[]{:S(2)}, u32[]{:S(2)}) collective-permute-start(f32[8,128]{1,0:T(8,128)S(1)} %broadcast_add_fusion), channel_id=1, source_target_pairs={{0,6},{1,7},{2,0},{3,1},{4,2},{5,3},{6,4},{7,5},{8,14},{9,15},{10,... | collective-permute-start | bytes 12296 | tf_op jit(solution)/shard_map/ppermute | solution.py:147
  170.7 4.0 %collective-permute-start.15 = (f32[8,128]{1,0:T(8,128)S(1)}, f32[8,128]{1,0:T(8,128)S(1)}, u32[]{:S(2)}, u32[]{:S(2)}) collective-permute-start(f32[8,128]{1,0:T(8,128)S(1)} %broadcast_add_fusion), channel_id=1, source_target_pairs={{0,4},{1,5},{2,6},{3,7},{4,0},{5,1},{6,2},{7,3},{8,12},{9,13},{10,... | collective-permute-start | bytes 12296 | tf_op jit(solution)/shard_map/ppermute | solution.py:147
  172.4 3.7 %collective-permute-start.14 = (f32[8,128]{1,0:T(8,128)S(1)}, f32[8,128]{1,0:T(8,128)S(1)}, u32[]{:S(2)}, u32[]{:S(2)}) collective-permute-start(f32[8,128]{1,0:T(8,128)S(1)} %broadcast_add_fusion), channel_id=1, source_target_pairs={{0,2},{1,3},{2,4},{3,5},{4,6},{5,7},{6,0},{7,1},{8,10},{9,11},{10,... | collective-permute-start | bytes 12296 | tf_op jit(solution)/shard_map/ppermute | solution.py:147
  176.8 8.4 %collective-permute-start.19 = (f32[8,128]{1,0:T(8,128)S(1)}, f32[8,128]{1,0:T(8,128)S(1)}, u32[]{:S(2)}, u32[]{:S(2)}) collective-permute-start(f32[8,128]{1,0:T(8,128)S(1)} %add_add_fusion.2), channel_id=1, source_target_pairs={{0,24},{1,25},{2,26},{3,27},{4,28},{5,29},{6,30},{7,31},{8,0},{9,1... | collective-permute-start | bytes 12296 | tf_op jit(solution)/shard_map/ppermute | solution.py:148
  177.7 7.5 %collective-permute-start.18 = (f32[8,128]{1,0:T(8,128)S(1)}, f32[8,128]{1,0:T(8,128)S(1)}, u32[]{:S(2)}, u32[]{:S(2)}) collective-permute-start(f32[8,128]{1,0:T(8,128)S(1)} %add_add_fusion.2), channel_id=1, source_target_pairs={{0,16},{1,17},{2,18},{3,19},{4,20},{5,21},{6,22},{7,23},{8,24},{9,... | collective-permute-start | bytes 12296 | tf_op jit(solution)/shard_map/ppermute | solution.py:148
  178.3 6.9 %collective-permute-start.17 = (f32[8,128]{1,0:T(8,128)S(1)}, f32[8,128]{1,0:T(8,128)S(1)}, u32[]{:S(2)}, u32[]{:S(2)}) collective-permute-start(f32[8,128]{1,0:T(8,128)S(1)} %add_add_fusion.2), channel_id=1, source_target_pairs={{0,8},{1,9},{2,10},{3,11},{4,12},{5,13},{6,14},{7,15},{8,16},{9,17... | collective-permute-start | bytes 12296 | tf_op jit(solution)/shard_map/ppermute | solution.py:148
  178.6 9.6 %copy-start.4 = (bf16[512,1024]{1,0:T(8,128)(2,1)S(1)}, bf16[512,1024]{1,0:T(8,128)(2,1)}, u32[]{:S(2)}) copy-start(bf16[512,1024]{1,0:T(8,128)(2,1)} %copy-done.3) | copy-start | bytes 3145732
  182.5 11.2 %collective-permute-start.3 = (f32[256,1024]{1,0:T(8,128)S(1)}, f32[256,1024]{1,0:T(8,128)S(1)}, u32[]{:S(2)}, u32[]{:S(2)}) collective-permute-start(f32[256,1024]{1,0:T(8,128)S(1)} %fusion.6), channel_id=1, source_target_pairs={{0,1},{1,0},{2,3},{3,2},{4,5},{5,4},{6,7},{7,6},{8,9},{9,8},{10,11... | collective-permute-start | bytes 3145736 | tf_op jit(solution)/shard_map/ppermute | solution.py:37
  185.2 4.3 %collective-permute-start.22 = (f32[8,128]{1,0:T(8,128)S(1)}, f32[8,128]{1,0:T(8,128)S(1)}, u32[]{:S(2)}, u32[]{:S(2)}) collective-permute-start(f32[8,128]{1,0:T(8,128)S(1)} %add_add_fusion.1), channel_id=1, source_target_pairs={{0,96},{32,0},{64,32},{96,64},{1,97},{33,1},{65,33},{97,65},{2,98}... | collective-permute-start | bytes 12296 | tf_op jit(solution)/shard_map/ppermute | solution.py:41
  185.5 4.0 %collective-permute-start.21 = (f32[8,128]{1,0:T(8,128)S(1)}, f32[8,128]{1,0:T(8,128)S(1)}, u32[]{:S(2)}, u32[]{:S(2)}) collective-permute-start(f32[8,128]{1,0:T(8,128)S(1)} %add_add_fusion.1), channel_id=1, source_target_pairs={{0,64},{32,96},{64,0},{96,32},{1,65},{33,97},{65,1},{97,33},{2,66}... | collective-permute-start | bytes 12296 | tf_op jit(solution)/shard_map/ppermute | solution.py:41
  188.2 3.7 %collective-permute-start.20 = (f32[8,128]{1,0:T(8,128)S(1)}, f32[8,128]{1,0:T(8,128)S(1)}, u32[]{:S(2)}, u32[]{:S(2)}) collective-permute-start(f32[8,128]{1,0:T(8,128)S(1)} %add_add_fusion.1), channel_id=1, source_target_pairs={{0,32},{32,64},{64,96},{96,0},{1,33},{33,65},{65,97},{97,1},{2,34}... | collective-permute-start | bytes 12296 | tf_op jit(solution)/shard_map/ppermute | solution.py:41
  (6 other events, 21.5 us)

commit v2 on v1

v2 whole, which is shorter than its diff:
```python
import functools

import jax
import jax.numpy as jnp
from jax import lax
from jax.experimental import pallas as pl
from jax.experimental.pallas import tpu as pltpu
from jax.sharding import PartitionSpec as P

D = 1024
HEADS = 16
HEAD_DIM = 64
PROJ = 256
DP = 4
CHIPS = 16
SEQ = "seq"
F32 = jnp.float32
BF16 = jnp.bfloat16
GROUP = 4
LOG2E = 1.4426950408889634


def place(y, z, core):
    return ((y % 4) * 4 + z % 4) * 2 + core % 2


def moved(dy, dz, dcore):
    return [
        (place(y, z, c), place(y + dy, z + dz, c + dcore))
        for y in range(4)
        for z in range(4)
        for c in range(2)
    ]


SAME_CORE = [[2 * chip + core for chip in range(CHIPS)] for core in range(2)]


def swap_cores(x):
    return lax.ppermute(x, SEQ, moved(0, 0, 1))


def along_x(x, step):
    return lax.ppermute(x, "dp", [(d, (d + step) % DP) for d in range(DP)])


def exchange_chips(x):
    return lax.all_to_all(x, SEQ, 0, 0, axis_index_groups=SAME_CORE)


def beside(x, *others):
    return lax.optimization_barrier((x, *others))


def scatter_rows(x):
    return exchange_chips(x.reshape(CHIPS, x.shape[0] // CHIPS, x.shape[1]))


def gather_sum(raw):
    copies = sum_copies(raw)
    rows = exchange_chips(copies)
    return rows.reshape(raw.shape[0] * raw.shape[1], raw.shape[2])


def dot_f32(form, left, right, precision=None):
    return jnp.einsum(form, left, right, preferred_element_type=F32, precision=precision)


def mm(left, right, left_dim, right_dim):
    return lax.dot_general(
        left, right, (((left_dim,), (right_dim,)), ((), ())), preferred_element_type=F32
    )


def attention_kernel(core_ref, query_ref, grad_ref, mine_ref, other_ref, att_ref, gq_ref, ours_ref, theirs_ref):
    first_core = core_ref[0] == 0
    mine, other = mine_ref[...], other_ref[...]
    keys = jnp.where(first_core, mine, other).astype(BF16)
    values = jnp.where(first_core, other, mine).astype(BF16)
    att, gq, gk, gv = [], [], [], []
    for h in range(GROUP):
        rows = slice(h * HEAD_DIM, (h + 1) * HEAD_DIM)
        query, grad, key, value = query_ref[rows, :], grad_ref[rows, :], keys[rows], values[rows]
        scores = mm(key, query, 0, 0)
        top = jnp.max(scores, axis=0, keepdims=True)
        raised = jnp.exp2((scores - top) * (0.125 * LOG2E))
        probs = raised * (1.0 / jnp.sum(raised, axis=0, keepdims=True))
        low = probs.astype(BF16)
        dprobs = mm(value * BF16(0.125), grad, 0, 0)
        inner = jnp.sum(dprobs * probs, axis=0, keepdims=True)
        dscores = (probs * (dprobs - inner)).astype(BF16)
        att.append(mm(value, low, 1, 0))
        gq.append(mm(key, dscores, 1, 0))
        gk.append(mm(query, dscores, 1, 1))
        gv.append(mm(grad, low, 1, 1))
    att_ref[...] = jnp.concatenate(att, axis=0).T.astype(BF16)
    gq_ref[...] = jnp.concatenate(gq, axis=0).T.astype(BF16)
    gk, gv = jnp.concatenate(gk, axis=0), jnp.concatenate(gv, axis=0)
    ours_ref[...] = jnp.where(first_core, gk, gv)
    theirs_ref[...] = jnp.where(first_core, gv, gk)


def attention(core, query_t, grad_t, mine_t, other_t):
    length = query_t.shape[1]
    wide = pl.BlockSpec((GROUP * HEAD_DIM, length), lambda i: (i, 0))
    narrow = pl.BlockSpec((GROUP * HEAD_DIM, PROJ), lambda i: (i, 0))
    tall = pl.BlockSpec((length, GROUP * HEAD_DIM), lambda i: (0, i))
    return pl.pallas_call(
        attention_kernel,
        grid=(HEADS // GROUP,),
        in_specs=[pl.BlockSpec(memory_space=pltpu.SMEM), wide, wide, narrow, narrow],
        out_specs=[tall, tall, narrow, narrow],
        out_shape=[
            jax.ShapeDtypeStruct((length, D), BF16),
            jax.ShapeDtypeStruct((length, D), BF16),
            jax.ShapeDtypeStruct((D, PROJ), F32),
            jax.ShapeDtypeStruct((D, PROJ), F32),
        ],
        compiler_params=pltpu.CompilerParams(vmem_limit_bytes=48 * 1024 * 1024),
        cost_estimate=pl.CostEstimate(
            flops=12 * length * PROJ * D, bytes_accessed=8 * 1024 * 1024, transcendentals=length * PROJ * HEADS
        ),
        name="attention",
    )(core, query_t, grad_t, mine_t, other_t)


def sum_copies_kernel(x_ref, out_ref):
    total = x_ref[0]
    for chip in range(1, CHIPS):
        total += x_ref[chip]
    for chip in range(CHIPS):
        out_ref[chip] = total


def sum_copies(x):
    return pl.pallas_call(
        sum_copies_kernel,
        out_shape=jax.ShapeDtypeStruct(x.shape, F32),
        cost_estimate=pl.CostEstimate(flops=x.size, bytes_accessed=8 * x.size, transcendentals=0),
        compiler_params=pltpu.CompilerParams(vmem_limit_bytes=32 * 1024 * 1024),
        name="sum_copies",
    )(x)


def grad_tokens_kernel(core_ref, first_ref, pk_ref, pv_ref, mine_ref, other_ref, out_ref):
    first_core = core_ref[0] == 0
    mine, other = mine_ref[...], other_ref[...]
    gk = jnp.where(first_core, mine, other).astype(BF16)
    gv = jnp.where(first_core, other, mine).astype(BF16)
    total = first_ref[...]
    total += mm(pk_ref[...], gk, 1, 1)
    total += mm(pv_ref[...], gv, 1, 1)
    out_ref[...] = total.astype(BF16)


def finish_tokens(core, first, pk_t, pv_t, mine_t, other_t):
    length = first.shape[0]
    tile = 256
    column = pl.BlockSpec((length, tile), lambda i: (0, i))
    row = pl.BlockSpec((tile, PROJ), lambda i: (i, 0))
    whole = pl.BlockSpec((length, PROJ), lambda i: (0, 0))
    return pl.pallas_call(
        grad_tokens_kernel,
        grid=(D // tile,),
        in_specs=[pl.BlockSpec(memory_space=pltpu.SMEM), column, whole, whole, row, row],
        out_specs=column,
        out_shape=jax.ShapeDtypeStruct((length, D), BF16),
        compiler_params=pltpu.CompilerParams(vmem_limit_bytes=32 * 1024 * 1024),
        cost_estimate=pl.CostEstimate(
            flops=1, bytes_accessed=1, transcendentals=0
        ),
        name="grad_tokens",
    )(core, first, pk_t, pv_t, mine_t, other_t)


def exchange_x(x):
    return lax.all_to_all(x, "dp", 0, 0)


def finish_sums_kernel(raw_ref, wkv_ref, wq_ref, squares_ref):
    total = raw_ref[0]
    for chip in range(1, CHIPS):
        total += raw_ref[chip]
    wq_ref[...] = total
    wkv = wkv_ref[...]
    rows = total.shape[0]
    squared = total * total + wkv[:rows] * wkv[:rows] + wkv[rows:] * wkv[rows:]
    squared = jnp.sum(jnp.sum(squared, axis=1, keepdims=True), axis=0, keepdims=True)
    squares_ref[...] = jnp.broadcast_to(squared[None], squares_ref.shape)


def finish_sums(raw, wkv):
    return pl.pallas_call(
        finish_sums_kernel,
        out_shape=[
            jax.ShapeDtypeStruct(raw.shape[1:], F32),
            jax.ShapeDtypeStruct((DP * CHIPS * 2, 1, 128), F32),
        ],
        cost_estimate=pl.CostEstimate(flops=raw.size, bytes_accessed=4 * raw.size, transcendentals=0),
        name="finish_sums",
    )(raw, wkv)


def clipped_kernel(squares_ref, wq_ref, wk_ref, wv_ref, out_ref):
    squared = jnp.sum(squares_ref[...], axis=0)[:, :1]
    clip = jnp.minimum(1.0, lax.rsqrt(squared + 1e-06))
    out_ref[:, :D] = wq_ref[...] * clip
    out_ref[:, D : 2 * D] = wk_ref[...] * clip
    out_ref[:, 2 * D :] = wv_ref[...] * clip


def clipped(squares, wq, wk, wv):
    return pl.pallas_call(
        clipped_kernel,
        out_shape=jax.ShapeDtypeStruct((wq.shape[0], 3 * D), F32),
        cost_estimate=pl.CostEstimate(flops=3 * wq.size, bytes_accessed=24 * wq.size, transcendentals=0),
        name="clipped",
    )(squares, wq, wk, wv)


def exact_kernel(left_ref, right_ref, out_ref, high_ref, middle_ref, low_ref):
    @pl.when(pl.program_id(0) == 0)
    def _():
        right = right_ref[...]
        high = right.astype(BF16)
        rest = right - high.astype(F32)
        middle = rest.astype(BF16)
        high_ref[...] = high
        middle_ref[...] = middle
        low_ref[...] = (rest - middle.astype(F32)).astype(BF16)

    left = left_ref[...]
    total = mm(left, low_ref[...], 1, 0)
    total += mm(left, middle_ref[...], 1, 0)
    out_ref[...] = total + mm(left, high_ref[...], 1, 0)


def exact_product(left, right):
    tile = 256
    return pl.pallas_call(
        exact_kernel,
        grid=(D // tile,),
        in_specs=[pl.BlockSpec((tile, D), lambda i: (i, 0)), pl.BlockSpec(right.shape, lambda i: (0, 0))],
        out_specs=pl.BlockSpec((tile, PROJ), lambda i: (i, 0)),
        out_shape=jax.ShapeDtypeStruct((D, PROJ), F32),
        scratch_shapes=[pltpu.VMEM(right.shape, BF16)] * 3,
        compiler_params=pltpu.CompilerParams(vmem_limit_bytes=32 * 1024 * 1024),
        cost_estimate=pl.CostEstimate(flops=1, bytes_accessed=1, transcendentals=0),
        name="exact_product",
    )(left, right)


def along_seq(x, dy, dz):
    return lax.ppermute(x, SEQ, moved(dy, dz, 0))


def per_device(tokens, w_query, w_key, w_value, proj_keys, proj_values, grad_out):
    inputs = tokens[0]
    upstream = grad_out[0]
    length = inputs.shape[0]
    seq_place, dp_place = lax.axis_index(SEQ), lax.axis_index("dp")
    core, chip = seq_place % 2, seq_place // 2
    y_place, z_place = chip // 4, chip % 4
    first_core = core == 0
    core_ref = core.reshape(1).astype(jnp.int32)
    rows = D // (DP * CHIPS * 2)
    quarter = CHIPS * rows
    pick = lambda x, at, axis: lax.dynamic_index_in_dim(x, at, axis, keepdims=False)

    theirs = jnp.where(first_core, proj_values, proj_keys)
    ours = jnp.where(first_core, proj_keys, proj_values)
    arrived = swap_cores(dot_f32("ps,sd->pd", theirs, inputs))
    part = dot_f32("ps,sd->pd", ours, inputs) + arrived
    raw = scatter_rows(part)

    upstream_t = upstream.T
    split = inputs.T.reshape(DP, CHIPS, 2, rows, length)
    mine = pick(split, core, 2).reshape(DP, quarter, length)
    other = pick(split, 1 - core, 2).reshape(DP, quarter, length)
    tokens_mine = [pick(mine, (dp_place + k) % DP, 0) for k in range(DP)]
    tokens_other = lax.dynamic_slice_in_dim(jnp.concatenate([other, other], axis=0), dp_place, DP, 0)
    tokens_other = tokens_other.reshape(DP * quarter, length)
    raw, upstream_t, tokens_mine, tokens_other = beside(raw, upstream_t, tokens_mine, tokens_other)
    my_tokens = gather_sum(raw)
    my_weight = jnp.where(first_core, w_key, w_value)
    query_t = dot_f32("sd,de->es", inputs, w_query).astype(BF16)
    my_tokens, my_weight, query_t, pk_t, pv_t = beside(my_tokens, my_weight, query_t, proj_keys.T, proj_values.T)
    my_proj_t = dot_f32("pe,ed->dp", my_tokens, my_weight.astype(F32), lax.Precision.HIGHEST)
    other_proj_t = swap_cores(my_proj_t)

    attended, grad_query, ours_t, theirs_t = attention(core_ref, query_t, upstream_t, my_proj_t, other_proj_t)

    part = ours_t + swap_cores(theirs_t)
    part, theirs = lax.optimization_barrier((part, dot_f32("cs,se->ce", tokens_other, grad_query)))
    raw = scatter_rows(part)
    arrived = swap_cores(theirs)
    wq = [
        dot_f32("cs,se->ce", tokens_mine[k], grad_query) + arrived[k * quarter : (k + 1) * quarter]
        for k in range(DP)
    ]
    half = quarter // 2
    up, down = along_x(wq[2][:half], 1), along_x(wq[2][half:], -1)
    ahead = jnp.concatenate([wq[1][:half] + up, wq[1][half:]], axis=0)
    behind = jnp.concatenate([wq[3][:half], wq[3][half:] + down], axis=0)
    raw, ahead, behind = beside(raw, ahead, behind)
    my_grad_t = gather_sum(raw)
    direct = dot_f32("se,de->sd", grad_query, w_query)
    columns = pick(my_tokens.reshape(PROJ, DP, CHIPS, 2 * rows), chip, 2)
    columns = jnp.concatenate([pick(columns, (dp_place + k) % DP, 1) for k in range(DP)], axis=1)
    wq = wq[0] + along_x(ahead, 1) + along_x(behind, -1)
    my_grad_t, wq, direct, columns = beside(my_grad_t, wq, direct, columns)

    raw = scatter_rows(wq)
    wkv = dot_f32("pc,ep->ce", columns, my_grad_t, lax.Precision.HIGHEST).reshape(DP, 2 * rows, D)
    wkv = wkv[0] + along_x(wkv[1], 1) + along_x(wkv[2], 2) + along_x(wkv[3], 3)
    my_grad_tokens_t = exact_product(my_weight, my_grad_t)
    raw, wkv, my_grad_tokens_t = beside(raw, wkv, my_grad_tokens_t)

    wq, squares = finish_sums(raw, wkv)
    squares = lax.all_to_all(squares, ("dp", SEQ), 0, 0)
    other_grad_tokens_t = swap_cores(my_grad_tokens_t)
    grad_tokens = finish_tokens(core_ref, direct, pk_t, pv_t, my_grad_tokens_t, other_grad_tokens_t)
    low, high = wkv[:rows], wkv[rows:]
    mine = jnp.where(first_core, low, high)
    arrived = swap_cores(jnp.where(first_core, high, low))
    wk = jnp.where(first_core, mine, arrived)
    wv = jnp.where(first_core, arrived, mine)
    squares, wk, wv, grad_tokens = beside(squares, wk, wv, grad_tokens)
    return (attended[None], grad_tokens[None], clipped(squares, wq, wk, wv))


def solution(mesh):
    return jax.shard_map(
        per_device,
        mesh=mesh,
        in_specs=(
            P("dp", "seq", None),
            P(),
            P(),
            P(),
            P(None, "seq"),
            P(None, "seq"),
            P("dp", "seq", None),
        ),
        out_specs=(P("dp", "seq", None), P("dp", "seq", None), P(("dp", "seq"), None)),
        check_vma=False,
    )
```

time: 198 us -> 172 us (0.87)
  blocking collectives: 42.2 us -> 0 us
  other arithmetic: 17.3 us -> 6.88 us
  Pallas kernels: 16.8 us -> 25.6 us
  starting transfers between devices: 49.2 us -> 56 us
  waiting for transfers between devices: 31.7 us -> 37.4 us
  matrix products: 18.7 us -> 23.4 us
    all_to_all x2 -> x0, blocking collectives: 42.2 us -> none  [exchange_chips(): return lax.all_to_all(x, SEQ, 0, 0, axis_index_groups=SAME_CORE)]
    all_to_all x3 -> x5, starting transfers between devices: 15.5 us -> 28.1 us  [exchange_chips(): return lax.all_to_all(x, SEQ, 0, 0, axis_index_groups=SAME_CORE)]
    unnamed x25 -> x46, local copies, waits for them, and re-layouts: 4.73 us -> 15.2 us
    pallas_call x2 -> x7, Pallas kernels: 16.8 us -> 25.6 us  [the longest x1 12.7 us: attention(): pl.pallas_call(attention_kernel, grid=(HEADS // GROUP,), in_specs=[pl.Blo...]
    all_to_all x0 -> x1, starting transfers between devices: none -> 8.8 us  [per_device(): squares = lax.all_to_all(squares, ('dp', SEQ), 0, 0)]
    ppermute x7 -> x6, starting transfers between devices: 17.3 us -> 10.2 us  [swap_cores(): return lax.ppermute(x, SEQ, moved(0, 0, 1))]
    add x8 -> x3, other arithmetic: 7.52 us -> 1.17 us  [the longest x1 1.1 us: per_device(): part = ours_t + swap_cores(theirs_t)]
    ppermute x10 -> x7, waiting for transfers between devices: 6.47 us -> 12.8 us  [along_x(): return lax.ppermute(x, 'dp', [(d, (d + step) % DP) for d in range(DP)])]
  transfers between devices with their start and end apart: 26 -> 19, of which waited for: 10 -> 10; matrix products, arithmetic and copies ran while one was open for 19% -> 20% of each run, Pallas kernels for 0% -> 6%
where the time goes in v2:
time: 172 us; the launch traced here: 171 us
  starting transfers between devices  56 us (33%)
  waiting for transfers between devices  37.4 us (22%)
  Pallas kernels  25.6 us (15%)
  matrix products  23.4 us (14%)
  local copies, waits for them, and re-layouts  20.7 us (12%)
  other arithmetic  6.88 us (4%)
    all_to_all x5, starting transfers between devices, exchange_chips(): return lax.all_to_all(x, SEQ, 0, 0, axis_index_groups=SAME_CORE)  28.1 us
    dot_general x11, matrix products, dot_f32(): jnp.einsum(form, left, right, preferred_element_type=F32, precision=preci...  23.4 us
    all_to_all x5, waiting for transfers between devices, exchange_chips(): return lax.all_to_all(x, SEQ, 0, 0, axis_index_groups=SAME_CORE)  18.5 us
    unnamed x46, local copies, waits for them, and re-layouts  15.2 us
    ppermute x7, waiting for transfers between devices, along_x(): return lax.ppermute(x, 'dp', [(d, (d + step) % DP) for d in range(DP)])  12.8 us
    pallas_call x1, Pallas kernels, attention(): pl.pallas_call(attention_kernel, grid=(HEADS // GROUP,), in_specs=[pl.Blo...  12.7 us
    ppermute x6, starting transfers between devices, swap_cores(): return lax.ppermute(x, SEQ, moved(0, 0, 1))  10.2 us
    ppermute x7, starting transfers between devices, along_x(): return lax.ppermute(x, 'dp', [(d, (d + step) % DP) for d in range(DP)])  8.95 us
  transfers between devices with their start and end apart: 19, of which 10 were waited for; matrix products, arithmetic and copies ran while one was open for 20% of the time, Pallas kernels for 6%

profile of v2, /device:TPU:1, one launch (start us, length us, event | category | flops | bytes accessed | tf_op | source)
XLA Modules:
  0.0 171.0 jit_solution(9772682528268792844)
XLA Ops:
  0.7 1.9 %fusion.3 = f32[256,1024]{1,0:T(8,128)S(1)} fusion(bf16[1,512,1024]{2,1,0:T(8,128)(2,1)} %param.7, bf16[256,512]{1,0:T(8,128)(2,1)} %param.12, bf16[256,512]{1,0:T(8,128)(2,1)} %param.11, pred[]{:T(512)S(6)} %eq.13), kind=kOutput, calls=%fused_computation.12 | convolution fusion | flops 268566528 | bytes 2621441 | tf_op jit(solution)/shard_map/ps,sd->pd/dot_general | solution.py:66
  4.1 2.3 %collective-permute-done = f32[256,1024]{1,0:T(8,128)S(1)} collective-permute-done((f32[256,1024]{1,0:T(8,128)S(1)}, f32[256,1024]{1,0:T(8,128)S(1)}, u32[]{:S(2)}, u32[]{:S(2)}) %collective-permute-start) | collective-permute-done | bytes 1048608 | tf_op jit(solution)/shard_map/ppermute | solution.py:40
  7.8 7.9 %all-to-all-start = ((f32[16,16,1024]{2,1,0:T(8,128)}), f32[16,16,1024]{2,1,0:T(8,128)S(1)}, u32[]{:S(2)}, u32[]{:S(2)}) async-start(f32[16,16,1024]{2,1,0:T(8,128)} %bitcast.71), calls=%async_computation | async-start | bytes 2097152 | tf_op jit(solution)/shard_map/all_to_all | solution.py:48
  15.7 2.3 %copy.13 = bf16[1,512,1024]{1,2,0:T(8,128)(2,1)} copy(bf16[1,512,1024]{2,1,0:T(8,128)(2,1)} %param.7) | data formatting | bytes 2097152 | tf_op args[0]
  18.0 2.3 %copy.14 = bf16[1,512,1024]{1,2,0:T(8,128)(2,1)} copy(bf16[1,512,1024]{2,1,0:T(8,128)(2,1)} %param.13) | data formatting | bytes 2097152 | tf_op args[6]
  23.3 7.3 %all-to-all-done.x_ref = f32[16,16,1024]{2,1,0:T(8,128)S(1)} async-done(((f32[16,16,1024]{2,1,0:T(8,128)}), f32[16,16,1024]{2,1,0:T(8,128)S(1)}, u32[]{:S(2)}, u32[]{:S(2)}) %all-to-all-start) | async-done | bytes 1048608 | tf_op jit(solution)/shard_map/all_to_all | solution.py:48
  31.8 5.3 %all-to-all-start.1 = ((f32[16,16,1024]{2,1,0:T(8,128)}), f32[16,16,1024]{2,1,0:T(8,128)}, u32[]{:S(2)}, u32[]{:S(2)}) async-start(f32[16,16,1024]{2,1,0:T(8,128)} %copy-done.3), calls=%async_computation.1 | async-start | bytes 2097152 | tf_op jit(solution)/shard_map/all_to_all | solution.py:48
  40.0 2.3 %convolution_convert_fusion.query_ref = bf16[1024,512]{1,0:T(8,128)(2,1)} fusion(bf16[1024,1024]{1,0:T(8,128)(2,1)S(1)} %copy-done, bf16[1,512,1024]{2,1,0:T(8,128)(2,1)S(1)} %copy-done.9), kind=kOutput, calls=%fused_computation.1 | convolution fusion | flops 1074266112 | bytes 4194304 | tf_op jit(solution)/shard_map/sd,de->es/dot_general | solution.py:66
  43.9 7.5 %all-to-all-done.1 = f32[16,16,1024]{2,1,0:T(8,128)} async-done(((f32[16,16,1024]{2,1,0:T(8,128)}), f32[16,16,1024]{2,1,0:T(8,128)}, u32[]{:S(2)}, u32[]{:S(2)}) %all-to-all-start.1) | async-done | bytes 1048608 | tf_op jit(solution)/shard_map/all_to_all | solution.py:48
  51.4 4.4 %fusion.16.mine_ref = f32[1024,256]{1,0:T(8,128)S(1)} fusion(bf16[1024,1024]{1,0:T(8,128)(2,1)} %broadcast_select_fusion.left_ref, f32[256,1024]{1,0:T(8,128)} %bitcast.16), kind=kOutput, calls=%fused_computation.45 | convolution fusion | flops 3221225472 | bytes 4194304 | tf_op jit(solution)/shard_map/pe,ed->dp/dot_general | solution.py:66
  55.8 3.9 %collective-permute-start.1 = (f32[1024,256]{1,0:T(8,128)S(1)}, f32[1024,256]{1,0:T(8,128)S(1)}, u32[]{:S(2)}, u32[]{:S(2)}) collective-permute-start(f32[1024,256]{1,0:T(8,128)S(1)} %fusion.16.mine_ref), channel_id=1, source_target_pairs={{0,1},{1,0},{2,3},{3,2},{4,5},{5,4},{6,7},{7,6},{8,9},{9,8},{10,11... | collective-permute-start | bytes 3145736 | tf_op jit(solution)/shard_map/ppermute | solution.py:40
  59.7 2.3 %collective-permute-done.1.other_ref = f32[1024,256]{1,0:T(8,128)S(1)} collective-permute-done((f32[1024,256]{1,0:T(8,128)S(1)}, f32[1024,256]{1,0:T(8,128)S(1)}, u32[]{:S(2)}, u32[]{:S(2)}) %collective-permute-start.1) | collective-permute-done | bytes 1048608 | tf_op jit(solution)/shard_map/ppermute | solution.py:40
  63.0 12.7 %attention.1 = (bf16[512,1024]{1,0:T(8,128)(2,1)}, bf16[512,1024]{1,0:T(8,128)(2,1)S(1)}, f32[1024,256]{1,0:T(8,128)S(1)}, f32[1024,256]{1,0:T(8,128)S(1)}) custom-call(s32[1]{0:T(128)} %bitcast.core_ref, bf16[1024,512]{1,0:T(8,128)(2,1)S(1)} %copy-done.7, bf16[1024,512]{1,0:T(8,128)(2,1)S(1)} %bitcast.68, f32[1024,256]{1,0:T(8,128)} %copy-done.16, ...), custom_call_target="tpu_custom_call" | custom-call | flops 1610612736 | bytes 8388608 | tf_op jit(solution)/shard_map/attention/pallas_call | solution.py:108
  76.1 2.1 %fusion.17 = f32[512,1024]{1,0:T(8,128)} fusion(bf16[512,512]{1,0:T(8,128)(2,1)S(1)} %bitcast.73, bf16[512,1024]{1,0:T(8,128)(2,1)S(1)} %get-tuple-element.46), kind=kOutput, calls=%fused_computation.46 | convolution fusion | flops 536870912 | bytes 3670016 | tf_op jit(solution)/shard_map/cs,se->ce/dot_general | solution.py:66
  79.8 4.4 %all-to-all-start.2 = ((f32[16,64,256]{2,1,0:T(8,128)}), f32[16,64,256]{2,1,0:T(8,128)}, u32[]{:S(2)}, u32[]{:S(2)}) async-start(f32[16,64,256]{2,1,0:T(8,128)} %bitcast.69), calls=%async_computation.2 | async-start | bytes 2097152 | tf_op jit(solution)/shard_map/all_to_all | solution.py:48
  85.8 2.5 %collective-permute-start.5 = (f32[64,1024]{1,0:T(8,128)S(1)}, f32[64,1024]{1,0:T(8,128)S(1)}, u32[]{:S(2)}, u32[]{:S(2)}) collective-permute-start(f32[64,1024]{1,0:T(8,128)S(1)} %get-tuple-element.79), channel_id=1, source_target_pairs={{0,96},{32,0},{64,32},{96,64},{1,97},{33,1},{65,33},{97,65},{2,98}... | collective-permute-start | bytes 786440 | tf_op jit(solution)/shard_map/ppermute | solution.py:44
  91.1 2.8 %collective-permute-done.5 = f32[64,1024]{1,0:T(8,128)S(1)} collective-permute-done((f32[64,1024]{1,0:T(8,128)S(1)}, f32[64,1024]{1,0:T(8,128)S(1)}, u32[]{:S(2)}, u32[]{:S(2)}) %collective-permute-start.5) | collective-permute-done | bytes 262176 | tf_op jit(solution)/shard_map/ppermute | solution.py:44
  93.9 3.0 %collective-permute-done.4 = f32[64,1024]{1,0:T(8,128)S(1)} collective-permute-done((f32[64,1024]{1,0:T(8,128)S(1)}, f32[64,1024]{1,0:T(8,128)S(1)}, u32[]{:S(2)}, u32[]{:S(2)}) %collective-permute-start.4) | collective-permute-done | bytes 262176 | tf_op jit(solution)/shard_map/ppermute | solution.py:44
  98.0 3.7 %all-to-all-done.2.x_ref = f32[16,64,256]{2,1,0:T(8,128)} async-done(((f32[16,64,256]{2,1,0:T(8,128)}), f32[16,64,256]{2,1,0:T(8,128)}, u32[]{:S(2)}, u32[]{:S(2)}) %all-to-all-start.2) | async-done | bytes 1048608 | tf_op jit(solution)/shard_map/all_to_all | solution.py:48
  104.1 4.4 %all-to-all-start.3 = ((f32[16,64,256]{2,1,0:T(8,128)}), f32[16,64,256]{2,1,0:T(8,128)}, u32[]{:S(2)}, u32[]{:S(2)}) async-start(f32[16,64,256]{2,1,0:T(8,128)} %copy-done.2), calls=%async_computation.3 | async-start | bytes 2097152 | tf_op jit(solution)/shard_map/all_to_all | solution.py:48
  108.5 2.6 %copy.17 = f32[256,1024]{0,1:T(8,128)} copy(f32[256,1024]{1,0:T(8,128)} %bitcast.16) | data formatting | bytes 2097152 | tf_op jit(solution)/shard_map/optimization_barrier | solution.py:52
  115.1 2.6 %fusion.18.first_ref = f32[512,1024]{1,0:T(8,128)} fusion(bf16[512,1024]{1,0:T(8,128)(2,1)S(1)} %get-tuple-element.46, bf16[1024,1024]{1,0:T(8,128)(2,1)S(1)} %copy-done), kind=kOutput, calls=%fused_computation.47 | convolution fusion | flops 1073741824 | bytes 5242880 | tf_op jit(solution)/shard_map/se,de->sd/dot_general | solution.py:66
  117.8 6.9 %collective-permute-done.6 = f32[128,1024]{1,0:T(8,128)S(1)} collective-permute-done((f32[128,1024]{1,0:T(8,128)}, f32[128,1024]{1,0:T(8,128)S(1)}, u32[]{:S(2)}, u32[]{:S(2)}) %collective-permute-start.6) | collective-permute-done | bytes 524320 | tf_op jit(solution)/shard_map/ppermute | solution.py:44
  124.7 2.1 %fusion.1 = f32[128,1024]{1,0:T(8,128)} fusion(f32[128,1024]{1,0:T(8,128)S(1)} %collective-permute-done.7, f32[128,1024]{1,0:T(8,128)S(1)} %collective-permute-done.6, bf16[128,512]{1,0:T(8,128)(2,1)S(1)} %get-tuple-element.53, bf16[512,1024]{1,0:T(8,128)(2,1)S(1)} %get-tuple-element.46, f32[512,1024]{1,0:T(8,128)} %collective-permute-done.3), kind=kOutput, calls=%fused_computation.8 | convolution fusion | flops 134610944 | bytes 3276800 | tf_op jit(solution)/shard_map/cs,se->ce/dot_general | solution.py:66
  126.8 6.2 %all-to-all-start.4 = ((f32[16,8,1024]{2,1,0:T(8,128)}), f32[16,8,1024]{2,1,0:T(8,128)}, u32[]{:S(2)}, u32[]{:S(2)}) async-start(f32[16,8,1024]{2,1,0:T(8,128)} %bitcast.72), calls=%async_computation.4 | async-start | bytes 1048576 | tf_op jit(solution)/shard_map/all_to_all | solution.py:48
  133.0 2.4 %fusion.19 = f32[64,1024]{1,0:T(8,128)S(1)} fusion(f32[256,64]{0,1:T(8,128)} %pad_maximum_fusion.2, f32[1024,256]{1,0:T(8,128)} %bitcast.21.right_ref), kind=kOutput, calls=%fused_computation.48 | convolution fusion | flops 201326592 | bytes 1376256 | tf_op jit(solution)/shard_map/pc,ep->ce/dot_general | solution.py:66
  135.4 2.5 %collective-permute-start.10 = (f32[16,1024]{1,0:T(8,128)S(1)}, f32[16,1024]{1,0:T(8,128)S(1)}, u32[]{:S(2)}, u32[]{:S(2)}) collective-permute-start(f32[16,1024]{1,0:T(8,128)S(1)} %get-tuple-element.88), channel_id=1, source_target_pairs={{0,96},{32,0},{64,32},{96,64},{1,97},{33,1},{65,33},{97,65},{2,98}... | collective-permute-start | bytes 196616 | tf_op jit(solution)/shard_map/ppermute | solution.py:44
  140.7 3.8 %exact_product.1.mine_ref = f32[1024,256]{1,0:T(8,128)S(1)} custom-call(bf16[1024,1024]{1,0:T(8,128)(2,1)S(1)} %copy-done.1, f32[1024,256]{1,0:T(8,128)} %bitcast.21.right_ref), custom_call_target="tpu_custom_call" | custom-call | flops 1 | bytes 1 | tf_op jit(solution)/shard_map/exact_product/pallas_call | solution.py:240
  144.6 4.0 %collective-permute-start.12 = (f32[1024,256]{1,0:T(8,128)S(1)}, f32[1024,256]{1,0:T(8,128)}, u32[]{:S(2)}, u32[]{:S(2)}) collective-permute-start(f32[1024,256]{1,0:T(8,128)S(1)} %exact_product.1.mine_ref), channel_id=1, source_target_pairs={{0,1},{1,0},{2,3},{3,2},{4,5},{5,4},{6,7},{7,6},{8,9},{9,8},{10,11... | collective-permute-start | bytes 3145736 | tf_op jit(solution)/shard_map/ppermute | solution.py:40
  148.7 1.8 %finish_sums.1 = (f32[8,1024]{1,0:T(8,128)}, f32[128,1,128]{2,1,0:T(1,128)}) custom-call(f32[16,8,1024]{2,1,0:T(8,128)} %all-to-all-done.4.raw_ref, f32[16,1024]{1,0:T(8,128)} %copy-done.15), custom_call_target="tpu_custom_call" | custom-call | flops 131072 | bytes 524288 | tf_op jit(solution)/shard_map/finish_sums/pallas_call | solution.py:193
  150.5 8.8 %all-to-all-start.5 = ((f32[128,1,128]{2,1,0:T(1,128)}), f32[128,1,128]{2,1,0:T(1,128)S(1)}, u32[]{:S(2)}, u32[]{:S(2)}) async-start(f32[128,1,128]{2,1,0:T(1,128)} %get-tuple-element.61), calls=%async_computation.5 | async-start | bytes 131072 | tf_op jit(solution)/shard_map/all_to_all | solution.py:320
  163.3 4.1 %grad_tokens.1 = bf16[512,1024]{1,0:T(8,128)(2,1)} custom-call(s32[1]{0:T(128)} %bitcast.core_ref, f32[512,1024]{1,0:T(8,128)S(1)} %copy-done.4, bf16[512,256]{1,0:T(8,128)(2,1)S(1)} %bitcast.66, bf16[512,256]{1,0:T(8,128)(2,1)S(1)} %bitcast.67, f32[1024,256]{1,0:T(8,128)S(1)} %exact_product.1.mine_ref, f32[1024,256]{1,0:T(8,128)} %collective-permute-done.12.other_ref), custom_call_target="tpu_custom_call" | custom-call | flops 1 | bytes 1 | tf_op jit(solution)/shard_map/grad_tokens/pallas_call | solution.py:162
  (86 shorter events, 37.0 us)
Async XLA Ops:
  0.6 39.4 %copy-start = (bf16[1024,1024]{1,0:T(8,128)(2,1)S(1)}, bf16[1024,1024]{1,0:T(8,128)(2,1)}, u32[]{:S(2)}) copy-start(bf16[1024,1024]{1,0:T(8,128)(2,1)} %param.8) | copy-start | bytes 6291460
  0.6 5.7 %copy-start.8 = (bf16[1,512,1024]{2,1,0:T(8,128)(2,1)S(1)}, bf16[1,512,1024]{2,1,0:T(8,128)(2,1)}, u32[]{:S(2)}) copy-start(bf16[1,512,1024]{2,1,0:T(8,128)(2,1)} %param.7) | copy-start | bytes 3145732
  0.7 5.7 %copy-start.10 = (bf16[256,512]{1,0:T(8,128)(2,1)S(1)}, bf16[256,512]{1,0:T(8,128)(2,1)}, u32[]{:S(2)}) copy-start(bf16[256,512]{1,0:T(8,128)(2,1)} %param.11) | copy-start | bytes 786436
  0.7 5.7 %copy-start.11 = (bf16[256,512]{1,0:T(8,128)(2,1)S(1)}, bf16[256,512]{1,0:T(8,128)(2,1)}, u32[]{:S(2)}) copy-start(bf16[256,512]{1,0:T(8,128)(2,1)} %param.12) | copy-start | bytes 786436
  2.6 3.8 %collective-permute-start = (f32[256,1024]{1,0:T(8,128)S(1)}, f32[256,1024]{1,0:T(8,128)S(1)}, u32[]{:S(2)}, u32[]{:S(2)}) collective-permute-start(f32[256,1024]{1,0:T(8,128)S(1)} %fusion.3), channel_id=1, source_target_pairs={{0,1},{1,0},{2,3},{3,2},{4,5},{5,4},{6,7},{7,6},{8,9},{9,8},{10,11... | collective-permute-start | bytes 3145736 | tf_op jit(solution)/shard_map/ppermute | solution.py:40
  7.8 22.9 %all-to-all-start = ((f32[16,16,1024]{2,1,0:T(8,128)}), f32[16,16,1024]{2,1,0:T(8,128)S(1)}, u32[]{:S(2)}, u32[]{:S(2)}) async-start(f32[16,16,1024]{2,1,0:T(8,128)} %bitcast.71), calls=%async_computation | async-start | bytes 2097152 | tf_op jit(solution)/shard_map/all_to_all | solution.py:48
  31.8 8.2 %copy-start.9 = (bf16[1,512,1024]{2,1,0:T(8,128)(2,1)S(1)}, bf16[1,512,1024]{2,1,0:T(8,128)(2,1)}, u32[]{:S(2)}) copy-start(bf16[1,512,1024]{2,1,0:T(8,128)(2,1)} %param.7) | copy-start | bytes 3145732
  31.8 19.6 %all-to-all-start.1 = ((f32[16,16,1024]{2,1,0:T(8,128)}), f32[16,16,1024]{2,1,0:T(8,128)}, u32[]{:S(2)}, u32[]{:S(2)}) async-start(f32[16,16,1024]{2,1,0:T(8,128)} %copy-done.3), calls=%async_computation.1 | async-start | bytes 2097152 | tf_op jit(solution)/shard_map/all_to_all | solution.py:48
  40.0 2.3 %copy-start.13 = (bf16[1024,1024]{1,0:T(8,128)(2,1)S(1)}, bf16[1024,1024]{1,0:T(8,128)(2,1)}, u32[]{:S(2)}) copy-start(bf16[1024,1024]{1,0:T(8,128)(2,1)} %param.10) | copy-start | bytes 6291460
  51.4 11.6 %copy-start.6 = (bf16[1,512,1024]{1,2,0:T(8,128)(2,1)S(1)}, bf16[1,512,1024]{1,2,0:T(8,128)(2,1)}, u32[]{:S(2)}) copy-start(bf16[1,512,1024]{1,2,0:T(8,128)(2,1)} %copy.14) | copy-start | bytes 3145732
  51.4 11.6 %copy-start.7 = (bf16[1024,512]{1,0:T(8,128)(2,1)S(1)}, bf16[1024,512]{1,0:T(8,128)(2,1)}, u32[]{:S(2)}) copy-start(bf16[1024,512]{1,0:T(8,128)(2,1)} %convolution_convert_fusion.query_ref) | copy-start | bytes 3145732
  55.8 6.2 %copy-start.16 = (f32[1024,256]{1,0:T(8,128)}, f32[1024,256]{1,0:T(8,128)S(1)}, u32[]{:S(2)}) copy-start(f32[1024,256]{1,0:T(8,128)S(1)} %fusion.16.mine_ref) | copy-start | bytes 3145732
  55.8 6.2 %collective-permute-start.1 = (f32[1024,256]{1,0:T(8,128)S(1)}, f32[1024,256]{1,0:T(8,128)S(1)}, u32[]{:S(2)}, u32[]{:S(2)}) collective-permute-start(f32[1024,256]{1,0:T(8,128)S(1)} %fusion.16.mine_ref), channel_id=1, source_target_pairs={{0,1},{1,0},{2,3},{3,2},{4,5},{5,4},{6,7},{7,6},{8,9},{9,8},{10,11... | collective-permute-start | bytes 3145736 | tf_op jit(solution)/shard_map/ppermute | solution.py:40
  63.0 13.1 %copy-start.14 = (bf16[4,128,512]{2,1,0:T(8,128)(2,1)S(1)}, bf16[4,128,512]{2,1,0:T(8,128)(2,1)}, u32[]{:S(2)}) copy-start(bf16[4,128,512]{2,1,0:T(8,128)(2,1)} %fusion.6) | copy-start | bytes 1572868
  75.7 2.7 %collective-permute-start.2 = (f32[1024,256]{1,0:T(8,128)S(1)}, f32[1024,256]{1,0:T(8,128)S(1)}, u32[]{:S(2)}, u32[]{:S(2)}) collective-permute-start(f32[1024,256]{1,0:T(8,128)S(1)} %get-tuple-element.44), channel_id=1, source_target_pairs={{0,1},{1,0},{2,3},{3,2},{4,5},{5,4},{6,7},{7,6},{8,9},{9,8},{10,11... | collective-permute-start | bytes 3145736 | tf_op jit(solution)/shard_map/ppermute | solution.py:40
  79.5 4.8 %collective-permute-start.3 = (f32[512,1024]{1,0:T(8,128)}, f32[512,1024]{1,0:T(8,128)}, u32[]{:S(2)}, u32[]{:S(2)}) collective-permute-start(f32[512,1024]{1,0:T(8,128)} %fusion.17), channel_id=1, source_target_pairs={{0,1},{1,0},{2,3},{3,2},{4,5},{5,4},{6,7},{7,6},{8,9},{9,8},{10,11... | collective-permute-start | bytes 6291464 | tf_op jit(solution)/shard_map/ppermute | solution.py:40
  79.8 21.9 %all-to-all-start.2 = ((f32[16,64,256]{2,1,0:T(8,128)}), f32[16,64,256]{2,1,0:T(8,128)}, u32[]{:S(2)}, u32[]{:S(2)}) async-start(f32[16,64,256]{2,1,0:T(8,128)} %bitcast.69), calls=%async_computation.2 | async-start | bytes 2097152 | tf_op jit(solution)/shard_map/all_to_all | solution.py:48
  84.2 4.1 %copy-start.18 = (bf16[128,512]{1,0:T(8,128)(2,1)S(1)}, bf16[128,512]{1,0:T(8,128)(2,1)}, u32[]{:S(2)}) copy-start(bf16[128,512]{1,0:T(8,128)(2,1)} %get-tuple-element.51) | copy-start | bytes 393220
  85.7 4.0 %copy-start.17 = (bf16[128,512]{1,0:T(8,128)(2,1)S(1)}, bf16[128,512]{1,0:T(8,128)(2,1)}, u32[]{:S(2)}) copy-start(bf16[128,512]{1,0:T(8,128)(2,1)} %get-tuple-element.48) | copy-start | bytes 393220
  85.8 8.1 %collective-permute-start.5 = (f32[64,1024]{1,0:T(8,128)S(1)}, f32[64,1024]{1,0:T(8,128)S(1)}, u32[]{:S(2)}, u32[]{:S(2)}) collective-permute-start(f32[64,1024]{1,0:T(8,128)S(1)} %get-tuple-element.79), channel_id=1, source_target_pairs={{0,96},{32,0},{64,32},{96,64},{1,97},{33,1},{65,33},{97,65},{2,98}... | collective-permute-start | bytes 786440 | tf_op jit(solution)/shard_map/ppermute | solution.py:44
  88.3 8.7 %collective-permute-start.4 = (f32[64,1024]{1,0:T(8,128)S(1)}, f32[64,1024]{1,0:T(8,128)S(1)}, u32[]{:S(2)}, u32[]{:S(2)}) collective-permute-start(f32[64,1024]{1,0:T(8,128)S(1)} %get-tuple-element.80), channel_id=1, source_target_pairs={{0,32},{32,64},{64,96},{96,0},{1,33},{33,65},{65,97},{97,1},{2,34}... | collective-permute-start | bytes 786440 | tf_op jit(solution)/shard_map/ppermute | solution.py:44
  104.1 22.8 %all-to-all-start.3 = ((f32[16,64,256]{2,1,0:T(8,128)}), f32[16,64,256]{2,1,0:T(8,128)}, u32[]{:S(2)}, u32[]{:S(2)}) async-start(f32[16,64,256]{2,1,0:T(8,128)} %copy-done.2), calls=%async_computation.3 | async-start | bytes 2097152 | tf_op jit(solution)/shard_map/all_to_all | solution.py:48
  111.0 13.6 %collective-permute-start.6 = (f32[128,1024]{1,0:T(8,128)}, f32[128,1024]{1,0:T(8,128)S(1)}, u32[]{:S(2)}, u32[]{:S(2)}) collective-permute-start(f32[128,1024]{1,0:T(8,128)} %get-tuple-element.54), channel_id=1, source_target_pairs={{0,32},{32,64},{64,96},{96,0},{1,33},{33,65},{65,97},{97,1},{2,34}... | collective-permute-start | bytes 1572872 | tf_op jit(solution)/shard_map/ppermute | solution.py:44
  112.2 12.4 %collective-permute-start.7 = (f32[128,1024]{1,0:T(8,128)}, f32[128,1024]{1,0:T(8,128)S(1)}, u32[]{:S(2)}, u32[]{:S(2)}) collective-permute-start(f32[128,1024]{1,0:T(8,128)} %get-tuple-element.55), channel_id=1, source_target_pairs={{0,96},{32,0},{64,32},{96,64},{1,97},{33,1},{65,33},{97,65},{2,98}... | collective-permute-start | bytes 1572872 | tf_op jit(solution)/shard_map/ppermute | solution.py:44
  126.8 17.8 %all-to-all-start.4 = ((f32[16,8,1024]{2,1,0:T(8,128)}), f32[16,8,1024]{2,1,0:T(8,128)}, u32[]{:S(2)}, u32[]{:S(2)}) async-start(f32[16,8,1024]{2,1,0:T(8,128)} %bitcast.72), calls=%async_computation.4 | async-start | bytes 1048576 | tf_op jit(solution)/shard_map/all_to_all | solution.py:48
  135.4 9.2 %collective-permute-start.10 = (f32[16,1024]{1,0:T(8,128)S(1)}, f32[16,1024]{1,0:T(8,128)S(1)}, u32[]{:S(2)}, u32[]{:S(2)}) collective-permute-start(f32[16,1024]{1,0:T(8,128)S(1)} %get-tuple-element.88), channel_id=1, source_target_pairs={{0,96},{32,0},{64,32},{96,64},{1,97},{33,1},{65,33},{97,65},{2,98}... | collective-permute-start | bytes 196616 | tf_op jit(solution)/shard_map/ppermute | solution.py:44
  137.8 6.7 %collective-permute-start.8 = (f32[16,1024]{1,0:T(8,128)S(1)}, f32[16,1024]{1,0:T(8,128)S(1)}, u32[]{:S(2)}, u32[]{:S(2)}) collective-permute-start(f32[16,1024]{1,0:T(8,128)S(1)} %get-tuple-element.87), channel_id=1, source_target_pairs={{0,32},{32,64},{64,96},{96,0},{1,33},{33,65},{65,97},{97,1},{2,34}... | collective-permute-start | bytes 196616 | tf_op jit(solution)/shard_map/ppermute | solution.py:44
  137.8 6.7 %collective-permute-start.9 = (f32[16,1024]{1,0:T(8,128)S(1)}, f32[16,1024]{1,0:T(8,128)S(1)}, u32[]{:S(2)}, u32[]{:S(2)}) collective-permute-start(f32[16,1024]{1,0:T(8,128)S(1)} %get-tuple-element.89), channel_id=1, source_target_pairs={{0,64},{32,96},{64,0},{96,32},{1,65},{33,97},{65,1},{97,33},{2,66}... | collective-permute-start | bytes 196616 | tf_op jit(solution)/shard_map/ppermute | solution.py:44
  144.6 4.1 %copy-start.15 = (f32[16,1024]{1,0:T(8,128)}, f32[16,1024]{1,0:T(8,128)S(1)}, u32[]{:S(2)}) copy-start(f32[16,1024]{1,0:T(8,128)S(1)} %fusion.12.wkv_ref) | copy-start | bytes 196612
  144.6 16.1 %collective-permute-start.12 = (f32[1024,256]{1,0:T(8,128)S(1)}, f32[1024,256]{1,0:T(8,128)}, u32[]{:S(2)}, u32[]{:S(2)}) collective-permute-start(f32[1024,256]{1,0:T(8,128)S(1)} %exact_product.1.mine_ref), channel_id=1, source_target_pairs={{0,1},{1,0},{2,3},{3,2},{4,5},{5,4},{6,7},{7,6},{8,9},{9,8},{10,11... | collective-permute-start | bytes 3145736 | tf_op jit(solution)/shard_map/ppermute | solution.py:40
  148.6 10.7 %collective-permute-start.11 = (f32[8,1024]{1,0:T(8,128)S(1)}, f32[8,1024]{1,0:T(8,128)S(1)}, u32[]{:S(2)}, u32[]{:S(2)}) collective-permute-start(f32[8,1024]{1,0:T(8,128)S(1)} %slice_select_fusion), channel_id=1, source_target_pairs={{0,1},{1,0},{2,3},{3,2},{4,5},{5,4},{6,7},{7,6},{8,9},{9,8},{10,11... | collective-permute-start | bytes 98312 | tf_op jit(solution)/shard_map/ppermute | solution.py:40
  150.5 18.2 %all-to-all-start.5 = ((f32[128,1,128]{2,1,0:T(1,128)}), f32[128,1,128]{2,1,0:T(1,128)S(1)}, u32[]{:S(2)}, u32[]{:S(2)}) async-start(f32[128,1,128]{2,1,0:T(1,128)} %get-tuple-element.61), calls=%async_computation.5 | async-start | bytes 131072 | tf_op jit(solution)/shard_map/all_to_all | solution.py:320
  (8 other events, 10.0 us)

commit v3 on v2

--- a/solution.py
+++ b/solution.py
@@ -165,7 +165,7 @@
         in_specs=[pl.BlockSpec(memory_space=pltpu.SMEM), column, whole, whole, row, row],
         out_specs=column,
         out_shape=jax.ShapeDtypeStruct((length, D), BF16),
-        compiler_params=pltpu.CompilerParams(vmem_limit_bytes=32 * 1024 * 1024),
+        compiler_params=pltpu.CompilerParams(vmem_limit_bytes=56 * 1024 * 1024),
         cost_estimate=pl.CostEstimate(
             flops=1, bytes_accessed=1, transcendentals=0
         ),
@@ -201,21 +201,28 @@
     )(raw, wkv)
 
 
-def clipped_kernel(squares_ref, wq_ref, wk_ref, wv_ref, out_ref):
+def clipped_kernel(core_ref, squares_ref, wq_ref, wkv_ref, arrived_ref, out_ref):
+    first_core = core_ref[0] == 0
+    rows = wq_ref.shape[0]
     squared = jnp.sum(squares_ref[...], axis=0)[:, :1]
     clip = jnp.minimum(1.0, lax.rsqrt(squared + 1e-06))
+    mine = jnp.where(first_core, wkv_ref[:rows], wkv_ref[rows:]) * clip
+    arrived = arrived_ref[...] * clip
     out_ref[:, :D] = wq_ref[...] * clip
-    out_ref[:, D : 2 * D] = wk_ref[...] * clip
-    out_ref[:, 2 * D :] = wv_ref[...] * clip
-
-
-def clipped(squares, wq, wk, wv):
+    out_ref[:, D : 2 * D] = jnp.where(first_core, mine, arrived)
+    out_ref[:, 2 * D :] = jnp.where(first_core, arrived, mine)
+
+
+def clipped(core, squares, wq, wkv, arrived):
+    whole = pl.BlockSpec(memory_space=pltpu.VMEM)
     return pl.pallas_call(
         clipped_kernel,
+        in_specs=[pl.BlockSpec(memory_space=pltpu.SMEM), whole, whole, whole, whole],
+        out_specs=whole,
         out_shape=jax.ShapeDtypeStruct((wq.shape[0], 3 * D), F32),
         cost_estimate=pl.CostEstimate(flops=3 * wq.size, bytes_accessed=24 * wq.size, transcendentals=0),
         name="clipped",
-    )(squares, wq, wk, wv)
+    )(core, squares, wq, wkv, arrived)
 
 
 def exact_kernel(left_ref, right_ref, out_ref, high_ref, middle_ref, low_ref):
@@ -298,17 +305,18 @@
         dot_f32("cs,se->ce", tokens_mine[k], grad_query) + arrived[k * quarter : (k + 1) * quarter]
         for k in range(DP)
     ]
+    my_tokens, wq[3] = lax.optimization_barrier((my_tokens, wq[3]))
+    columns = pick(my_tokens.reshape(PROJ, DP, CHIPS, 2 * rows), chip, 2)
+    columns = jnp.concatenate([pick(columns, (dp_place + k) % DP, 1) for k in range(DP)], axis=1)
     half = quarter // 2
     up, down = along_x(wq[2][:half], 1), along_x(wq[2][half:], -1)
     ahead = jnp.concatenate([wq[1][:half] + up, wq[1][half:]], axis=0)
     behind = jnp.concatenate([wq[3][:half], wq[3][half:] + down], axis=0)
-    raw, ahead, behind = beside(raw, ahead, behind)
+    raw, ahead, behind, columns = beside(raw, ahead, behind, columns)
     my_grad_t = gather_sum(raw)
     direct = dot_f32("se,de->sd", grad_query, w_query)
-    columns = pick(my_tokens.reshape(PROJ, DP, CHIPS, 2 * rows), chip, 2)
-    columns = jnp.concatenate([pick(columns, (dp_place + k) % DP, 1) for k in range(DP)], axis=1)
     wq = wq[0] + along_x(ahead, 1) + along_x(behind, -1)
-    my_grad_t, wq, direct, columns = beside(my_grad_t, wq, direct, columns)
+    my_grad_t, wq, direct = beside(my_grad_t, wq, direct)
 
     raw = scatter_rows(wq)
     wkv = dot_f32("pc,ep->ce", columns, my_grad_t, lax.Precision.HIGHEST).reshape(DP, 2 * rows, D)
@@ -320,13 +328,9 @@
     squares = lax.all_to_all(squares, ("dp", SEQ), 0, 0)
     other_grad_tokens_t = swap_cores(my_grad_tokens_t)
     grad_tokens = finish_tokens(core_ref, direct, pk_t, pv_t, my_grad_tokens_t, other_grad_tokens_t)
-    low, high = wkv[:rows], wkv[rows:]
-    mine = jnp.where(first_core, low, high)
-    arrived = swap_cores(jnp.where(first_core, high, low))
-    wk = jnp.where(first_core, mine, arrived)
-    wv = jnp.where(first_core, arrived, mine)
-    squares, wk, wv, grad_tokens = beside(squares, wk, wv, grad_tokens)
-    return (attended[None], grad_tokens[None], clipped(squares, wq, wk, wv))
+    arrived = swap_cores(jnp.where(first_core, wkv[rows:], wkv[:rows]))
+    squares, arrived, grad_tokens = beside(squares, arrived, grad_tokens)
+    return (attended[None], grad_tokens[None], clipped(core_ref, squares, wq, wkv, arrived))
 
 
 def solution(mesh):

time: 172 us -> 171 us (level)
  waiting for transfers between devices: 37.4 us -> 32.1 us
  local copies, waits for them, and re-layouts: 20.7 us -> 18.6 us
    ppermute x7, waiting for transfers between devices: 12.8 us -> 8.02 us  [along_x(): return lax.ppermute(x, 'dp', [(d, (d + step) % DP) for d in range(DP)])]
    unnamed x46, local copies, waits for them, and re-layouts: 15.2 us -> 12.4 us
    all_to_all x5, waiting for transfers between devices: 18.5 us -> 16.7 us  [exchange_chips(): return lax.all_to_all(x, SEQ, 0, 0, axis_index_groups=SAME_CORE)]
  transfers between devices with their start and end apart: 19 -> 19, of which waited for: 10 -> 9; matrix products, arithmetic and copies ran while one was open for 20% -> 23% of each run, Pallas kernels for 6% -> 6%
where the time goes in v3:
time: 171 us; the launch traced here: 169 us
  starting transfers between devices  57.7 us (34%)
  waiting for transfers between devices  32.1 us (19%)
  Pallas kernels  26.4 us (15%)
  matrix products  25 us (15%)
  local copies, waits for them, and re-layouts  18.6 us (11%)
  other arithmetic  8.5 us (5%)
    all_to_all x5, starting transfers between devices, exchange_chips(): return lax.all_to_all(x, SEQ, 0, 0, axis_index_groups=SAME_CORE)  28.7 us
    dot_general x11, matrix products, dot_f32(): jnp.einsum(form, left, right, preferred_element_type=F32, precision=preci...  25 us
    all_to_all x5, waiting for transfers between devices, exchange_chips(): return lax.all_to_all(x, SEQ, 0, 0, axis_index_groups=SAME_CORE)  16.7 us
    pallas_call x1, Pallas kernels, attention(): pl.pallas_call(attention_kernel, grid=(HEADS // GROUP,), in_specs=[pl.Blo...  12.7 us
    unnamed x46, local copies, waits for them, and re-layouts  12.4 us
    ppermute x6, starting transfers between devices, swap_cores(): return lax.ppermute(x, SEQ, moved(0, 0, 1))  11 us
    ppermute x7, starting transfers between devices, along_x(): return lax.ppermute(x, 'dp', [(d, (d + step) % DP) for d in range(DP)])  9.62 us
    all_to_all x1, starting transfers between devices, per_device(): squares = lax.all_to_all(squares, ('dp', SEQ), 0, 0)  8.37 us
  transfers between devices with their start and end apart: 19, of which 9 were waited for; matrix products, arithmetic and copies ran while one was open for 23% of the time, Pallas kernels for 6%

profile of v3, /device:TPU:1, one launch (start us, length us, event | category | flops | bytes accessed | tf_op | source)
XLA Modules:
  0.0 169.2 jit_solution(9112060644170743899)
XLA Ops:
  0.7 1.9 %fusion.3 = f32[256,1024]{1,0:T(8,128)S(1)} fusion(bf16[1,512,1024]{2,1,0:T(8,128)(2,1)} %param.7, bf16[256,512]{1,0:T(8,128)(2,1)} %param.12, bf16[256,512]{1,0:T(8,128)(2,1)} %param.11, pred[]{:T(512)S(6)} %eq.13), kind=kOutput, calls=%fused_computation.12 | convolution fusion | flops 268566528 | bytes 2621441 | tf_op jit(solution)/shard_map/ps,sd->pd/dot_general | solution.py:66
  4.1 2.3 %collective-permute-done = f32[256,1024]{1,0:T(8,128)S(1)} collective-permute-done((f32[256,1024]{1,0:T(8,128)S(1)}, f32[256,1024]{1,0:T(8,128)S(1)}, u32[]{:S(2)}, u32[]{:S(2)}) %collective-permute-start) | collective-permute-done | bytes 1048608 | tf_op jit(solution)/shard_map/ppermute | solution.py:40
  7.8 7.9 %all-to-all-start = ((f32[16,16,1024]{2,1,0:T(8,128)}), f32[16,16,1024]{2,1,0:T(8,128)S(1)}, u32[]{:S(2)}, u32[]{:S(2)}) async-start(f32[16,16,1024]{2,1,0:T(8,128)} %bitcast.69), calls=%async_computation | async-start | bytes 2097152 | tf_op jit(solution)/shard_map/all_to_all | solution.py:48
  15.7 2.3 %copy.13 = bf16[1,512,1024]{1,2,0:T(8,128)(2,1)} copy(bf16[1,512,1024]{2,1,0:T(8,128)(2,1)} %param.7) | data formatting | bytes 2097152 | tf_op args[0]
  18.0 2.3 %copy.14 = bf16[1,512,1024]{1,2,0:T(8,128)(2,1)} copy(bf16[1,512,1024]{2,1,0:T(8,128)(2,1)} %param.13) | data formatting | bytes 2097152 | tf_op args[6]
  23.3 7.4 %all-to-all-done.x_ref = f32[16,16,1024]{2,1,0:T(8,128)S(1)} async-done(((f32[16,16,1024]{2,1,0:T(8,128)}), f32[16,16,1024]{2,1,0:T(8,128)S(1)}, u32[]{:S(2)}, u32[]{:S(2)}) %all-to-all-start) | async-done | bytes 1048608 | tf_op jit(solution)/shard_map/all_to_all | solution.py:48
  31.8 5.3 %all-to-all-start.1 = ((f32[16,16,1024]{2,1,0:T(8,128)}), f32[16,16,1024]{2,1,0:T(8,128)}, u32[]{:S(2)}, u32[]{:S(2)}) async-start(f32[16,16,1024]{2,1,0:T(8,128)} %copy-done.3), calls=%async_computation.1 | async-start | bytes 2097152 | tf_op jit(solution)/shard_map/all_to_all | solution.py:48
  39.7 2.3 %convolution_convert_fusion.query_ref = bf16[1024,512]{1,0:T(8,128)(2,1)} fusion(bf16[1024,1024]{1,0:T(8,128)(2,1)S(1)} %copy-done, bf16[1,512,1024]{2,1,0:T(8,128)(2,1)S(1)} %copy-done.8), kind=kOutput, calls=%fused_computation.1 | convolution fusion | flops 1074266112 | bytes 4194304 | tf_op jit(solution)/shard_map/sd,de->es/dot_general | solution.py:66
  43.6 7.8 %all-to-all-done.1 = f32[16,16,1024]{2,1,0:T(8,128)} async-done(((f32[16,16,1024]{2,1,0:T(8,128)}), f32[16,16,1024]{2,1,0:T(8,128)}, u32[]{:S(2)}, u32[]{:S(2)}) %all-to-all-start.1) | async-done | bytes 1048608 | tf_op jit(solution)/shard_map/all_to_all | solution.py:48
  51.4 4.4 %fusion.16.mine_ref = f32[1024,256]{1,0:T(8,128)S(1)} fusion(bf16[1024,1024]{1,0:T(8,128)(2,1)} %broadcast_select_fusion.left_ref, f32[256,1024]{1,0:T(8,128)} %bitcast.16), kind=kOutput, calls=%fused_computation.42 | convolution fusion | flops 3221225472 | bytes 4194304 | tf_op jit(solution)/shard_map/pe,ed->dp/dot_general | solution.py:66
  55.8 3.9 %collective-permute-start.1 = (f32[1024,256]{1,0:T(8,128)S(1)}, f32[1024,256]{1,0:T(8,128)S(1)}, u32[]{:S(2)}, u32[]{:S(2)}) collective-permute-start(f32[1024,256]{1,0:T(8,128)S(1)} %fusion.16.mine_ref), channel_id=1, source_target_pairs={{0,1},{1,0},{2,3},{3,2},{4,5},{5,4},{6,7},{7,6},{8,9},{9,8},{10,11... | collective-permute-start | bytes 3145736 | tf_op jit(solution)/shard_map/ppermute | solution.py:40
  59.7 2.3 %collective-permute-done.1.other_ref = f32[1024,256]{1,0:T(8,128)S(1)} collective-permute-done((f32[1024,256]{1,0:T(8,128)S(1)}, f32[1024,256]{1,0:T(8,128)S(1)}, u32[]{:S(2)}, u32[]{:S(2)}) %collective-permute-start.1) | collective-permute-done | bytes 1048608 | tf_op jit(solution)/shard_map/ppermute | solution.py:40
  63.0 12.7 %attention.1 = (bf16[512,1024]{1,0:T(8,128)(2,1)}, bf16[512,1024]{1,0:T(8,128)(2,1)S(1)}, f32[1024,256]{1,0:T(8,128)S(1)}, f32[1024,256]{1,0:T(8,128)S(1)}) custom-call(s32[1]{0:T(128)} %bitcast.core_ref, bf16[1024,512]{1,0:T(8,128)(2,1)S(1)} %copy-done.6, bf16[1024,512]{1,0:T(8,128)(2,1)S(1)} %bitcast.66, f32[1024,256]{1,0:T(8,128)} %copy-done.14, ...), custom_call_target="tpu_custom_call" | custom-call | flops 1610612736 | bytes 8388608 | tf_op jit(solution)/shard_map/attention/pallas_call | solution.py:108
  76.1 2.1 %fusion.17 = f32[512,1024]{1,0:T(8,128)} fusion(bf16[512,512]{1,0:T(8,128)(2,1)S(1)} %bitcast.71, bf16[512,1024]{1,0:T(8,128)(2,1)S(1)} %get-tuple-element.47), kind=kOutput, calls=%fused_computation.43 | convolution fusion | flops 536870912 | bytes 3670016 | tf_op jit(solution)/shard_map/cs,se->ce/dot_general | solution.py:66
  79.8 4.3 %all-to-all-start.2 = ((f32[16,64,256]{2,1,0:T(8,128)}), f32[16,64,256]{2,1,0:T(8,128)}, u32[]{:S(2)}, u32[]{:S(2)}) async-start(f32[16,64,256]{2,1,0:T(8,128)} %bitcast.67), calls=%async_computation.2 | async-start | bytes 2097152 | tf_op jit(solution)/shard_map/all_to_all | solution.py:48
  86.5 2.5 %collective-permute-start.5 = (f32[64,1024]{1,0:T(8,128)}, f32[64,1024]{1,0:T(8,128)}, u32[]{:S(2)}, u32[]{:S(2)}) collective-permute-start(f32[64,1024]{1,0:T(8,128)} %get-tuple-element.81), channel_id=1, source_target_pairs={{0,96},{32,0},{64,32},{96,64},{1,97},{33,1},{65,33},{97,65},{2,98}... | collective-permute-start | bytes 786440 | tf_op jit(solution)/shard_map/ppermute | solution.py:44
  89.0 2.2 %convolution_add_fusion.2 = f32[128,1024]{1,0:T(8,128)} fusion(bf16[128,512]{1,0:T(8,128)(2,1)S(1)} %copy-done.16, bf16[512,1024]{1,0:T(8,128)(2,1)S(1)} %get-tuple-element.47, f32[512,1024]{1,0:T(8,128)} %collective-permute-done.3), kind=kOutput, calls=%fused_computation.4 | convolution fusion | flops 134348800 | bytes 2228224 | tf_op jit(solution)/shard_map/cs,se->ce/dot_general | solution.py:66
  91.1 2.2 %convolution_add_fusion.4 = f32[128,1024]{1,0:T(8,128)} fusion(bf16[128,512]{1,0:T(8,128)(2,1)S(1)} %copy-done.15, bf16[512,1024]{1,0:T(8,128)(2,1)S(1)} %get-tuple-element.47, f32[512,1024]{1,0:T(8,128)} %collective-permute-done.3), kind=kOutput, calls=%fused_computation.6 | convolution fusion | flops 134348800 | bytes 2228224 | tf_op jit(solution)/shard_map/cs,se->ce/dot_general | solution.py:66
  93.3 2.5 %copy.17 = f32[256,1024]{0,1:T(8,128)} copy(f32[256,1024]{1,0:T(8,128)} %bitcast.16) | data formatting | bytes 2097152 | tf_op jit(solution)/shard_map/optimization_barrier | solution.py:308
  104.0 4.9 %all-to-all-start.3 = ((f32[16,64,256]{2,1,0:T(8,128)}), f32[16,64,256]{2,1,0:T(8,128)}, u32[]{:S(2)}, u32[]{:S(2)}) async-start(f32[16,64,256]{2,1,0:T(8,128)} %copy-done.2), calls=%async_computation.3 | async-start | bytes 2097152 | tf_op jit(solution)/shard_map/all_to_all | solution.py:48
  109.6 2.1 %collective-permute-start.7 = (f32[128,1024]{1,0:T(8,128)}, f32[128,1024]{1,0:T(8,128)S(1)}, u32[]{:S(2)}, u32[]{:S(2)}) collective-permute-start(f32[128,1024]{1,0:T(8,128)} %get-tuple-element.58), channel_id=1, source_target_pairs={{0,96},{32,0},{64,32},{96,64},{1,97},{33,1},{65,33},{97,65},{2,98}... | collective-permute-start | bytes 1572872 | tf_op jit(solution)/shard_map/ppermute | solution.py:44
  111.7 2.6 %fusion.18.first_ref = f32[512,1024]{1,0:T(8,128)} fusion(bf16[512,1024]{1,0:T(8,128)(2,1)S(1)} %get-tuple-element.47, bf16[1024,1024]{1,0:T(8,128)(2,1)S(1)} %copy-done), kind=kOutput, calls=%fused_computation.44 | convolution fusion | flops 1073741824 | bytes 5242880 | tf_op jit(solution)/shard_map/se,de->sd/dot_general | solution.py:66
  114.4 7.9 %collective-permute-done.6 = f32[128,1024]{1,0:T(8,128)S(1)} collective-permute-done((f32[128,1024]{1,0:T(8,128)}, f32[128,1024]{1,0:T(8,128)S(1)}, u32[]{:S(2)}, u32[]{:S(2)}) %collective-permute-start.6) | collective-permute-done | bytes 524320 | tf_op jit(solution)/shard_map/ppermute | solution.py:44
  122.2 2.2 %fusion.1 = f32[128,1024]{1,0:T(8,128)} fusion(f32[128,1024]{1,0:T(8,128)S(1)} %collective-permute-done.7, f32[128,1024]{1,0:T(8,128)S(1)} %collective-permute-done.6, bf16[128,512]{1,0:T(8,128)(2,1)S(1)} %get-tuple-element.56, bf16[512,1024]{1,0:T(8,128)(2,1)S(1)} %get-tuple-element.47, f32[512,1024]{1,0:T(8,128)} %collective-permute-done.3), kind=kOutput, calls=%fused_computation.8 | convolution fusion | flops 134610944 | bytes 3276800 | tf_op jit(solution)/shard_map/cs,se->ce/dot_general | solution.py:66
  124.4 6.3 %all-to-all-start.4 = ((f32[16,8,1024]{2,1,0:T(8,128)}), f32[16,8,1024]{2,1,0:T(8,128)}, u32[]{:S(2)}, u32[]{:S(2)}) async-start(f32[16,8,1024]{2,1,0:T(8,128)} %bitcast.70), calls=%async_computation.4 | async-start | bytes 1048576 | tf_op jit(solution)/shard_map/all_to_all | solution.py:48
  130.8 2.3 %fusion.19 = f32[64,1024]{1,0:T(8,128)S(1)} fusion(f32[256,64]{0,1:T(8,128)S(1)} %pad_maximum_fusion.2, f32[1024,256]{1,0:T(8,128)} %bitcast.26.right_ref), kind=kOutput, calls=%fused_computation.45 | convolution fusion | flops 201326592 | bytes 1376256 | tf_op jit(solution)/shard_map/pc,ep->ce/dot_general | solution.py:66
  133.1 2.6 %collective-permute-start.10 = (f32[16,1024]{1,0:T(8,128)S(1)}, f32[16,1024]{1,0:T(8,128)S(1)}, u32[]{:S(2)}, u32[]{:S(2)}) collective-permute-start(f32[16,1024]{1,0:T(8,128)S(1)} %get-tuple-element.90), channel_id=1, source_target_pairs={{0,96},{32,0},{64,32},{96,64},{1,97},{33,1},{65,33},{97,65},{2,98}... | collective-permute-start | bytes 196616 | tf_op jit(solution)/shard_map/ppermute | solution.py:44
  139.0 3.8 %exact_product.1.mine_ref = f32[1024,256]{1,0:T(8,128)S(1)} custom-call(bf16[1024,1024]{1,0:T(8,128)(2,1)S(1)} %copy-done.1, f32[1024,256]{1,0:T(8,128)} %bitcast.26.right_ref), custom_call_target="tpu_custom_call" | custom-call | flops 1 | bytes 1 | tf_op jit(solution)/shard_map/exact_product/pallas_call | solution.py:247
  143.6 3.8 %collective-permute-start.12 = (f32[1024,256]{1,0:T(8,128)S(1)}, f32[1024,256]{1,0:T(8,128)}, u32[]{:S(2)}, u32[]{:S(2)}) collective-permute-start(f32[1024,256]{1,0:T(8,128)S(1)} %exact_product.1.mine_ref), channel_id=1, source_target_pairs={{0,1},{1,0},{2,3},{3,2},{4,5},{5,4},{6,7},{7,6},{8,9},{9,8},{10,11... | collective-permute-start | bytes 3145736 | tf_op jit(solution)/shard_map/ppermute | solution.py:40
  149.2 8.4 %all-to-all-start.5 = ((f32[128,1,128]{2,1,0:T(1,128)}), f32[128,1,128]{2,1,0:T(1,128)S(1)}, u32[]{:S(2)}, u32[]{:S(2)}) async-start(f32[128,1,128]{2,1,0:T(1,128)} %get-tuple-element.64), calls=%async_computation.5 | async-start | bytes 131072 | tf_op jit(solution)/shard_map/all_to_all | solution.py:328
  159.4 4.8 %grad_tokens.1 = bf16[512,1024]{1,0:T(8,128)(2,1)} custom-call(s32[1]{0:T(128)} %bitcast.core_ref, f32[512,1024]{1,0:T(8,128)} %fusion.18.first_ref, bf16[512,256]{1,0:T(8,128)(2,1)} %bitcast.73, bf16[512,256]{1,0:T(8,128)(2,1)} %bitcast.74, f32[1024,256]{1,0:T(8,128)} %copy-done.4, f32[1024,256]{1,0:T(8,128)} %collective-permute-done.12.other_ref), custom_call_target="tpu_custom_call" | custom-call | flops 1 | bytes 1 | tf_op jit(solution)/shard_map/grad_tokens/pallas_call | solution.py:162
  164.2 2.6 %all-to-all-done.5.squares_ref = f32[128,1,128]{2,1,0:T(1,128)S(1)} async-done(((f32[128,1,128]{2,1,0:T(1,128)}), f32[128,1,128]{2,1,0:T(1,128)S(1)}, u32[]{:S(2)}, u32[]{:S(2)}) %all-to-all-start.5) | async-done | bytes 65568 | tf_op jit(solution)/shard_map/all_to_all | solution.py:328
  (85 shorter events, 35.5 us)
Async XLA Ops:
  0.6 39.1 %copy-start = (bf16[1024,1024]{1,0:T(8,128)(2,1)S(1)}, bf16[1024,1024]{1,0:T(8,128)(2,1)}, u32[]{:S(2)}) copy-start(bf16[1024,1024]{1,0:T(8,128)(2,1)} %param.8) | copy-start | bytes 6291460
  0.6 5.7 %copy-start.7 = (bf16[1,512,1024]{2,1,0:T(8,128)(2,1)S(1)}, bf16[1,512,1024]{2,1,0:T(8,128)(2,1)}, u32[]{:S(2)}) copy-start(bf16[1,512,1024]{2,1,0:T(8,128)(2,1)} %param.7) | copy-start | bytes 3145732
  0.7 5.7 %copy-start.9 = (bf16[256,512]{1,0:T(8,128)(2,1)S(1)}, bf16[256,512]{1,0:T(8,128)(2,1)}, u32[]{:S(2)}) copy-start(bf16[256,512]{1,0:T(8,128)(2,1)} %param.11) | copy-start | bytes 786436
  0.7 5.7 %copy-start.10 = (bf16[256,512]{1,0:T(8,128)(2,1)S(1)}, bf16[256,512]{1,0:T(8,128)(2,1)}, u32[]{:S(2)}) copy-start(bf16[256,512]{1,0:T(8,128)(2,1)} %param.12) | copy-start | bytes 786436
  2.6 3.8 %collective-permute-start = (f32[256,1024]{1,0:T(8,128)S(1)}, f32[256,1024]{1,0:T(8,128)S(1)}, u32[]{:S(2)}, u32[]{:S(2)}) collective-permute-start(f32[256,1024]{1,0:T(8,128)S(1)} %fusion.3), channel_id=1, source_target_pairs={{0,1},{1,0},{2,3},{3,2},{4,5},{5,4},{6,7},{7,6},{8,9},{9,8},{10,11... | collective-permute-start | bytes 3145736 | tf_op jit(solution)/shard_map/ppermute | solution.py:40
  7.8 22.9 %all-to-all-start = ((f32[16,16,1024]{2,1,0:T(8,128)}), f32[16,16,1024]{2,1,0:T(8,128)S(1)}, u32[]{:S(2)}, u32[]{:S(2)}) async-start(f32[16,16,1024]{2,1,0:T(8,128)} %bitcast.69), calls=%async_computation | async-start | bytes 2097152 | tf_op jit(solution)/shard_map/all_to_all | solution.py:48
  31.8 7.9 %copy-start.8 = (bf16[1,512,1024]{2,1,0:T(8,128)(2,1)S(1)}, bf16[1,512,1024]{2,1,0:T(8,128)(2,1)}, u32[]{:S(2)}) copy-start(bf16[1,512,1024]{2,1,0:T(8,128)(2,1)} %param.7) | copy-start | bytes 3145732
  31.8 19.6 %all-to-all-start.1 = ((f32[16,16,1024]{2,1,0:T(8,128)}), f32[16,16,1024]{2,1,0:T(8,128)}, u32[]{:S(2)}, u32[]{:S(2)}) async-start(f32[16,16,1024]{2,1,0:T(8,128)} %copy-done.3), calls=%async_computation.1 | async-start | bytes 2097152 | tf_op jit(solution)/shard_map/all_to_all | solution.py:48
  51.4 11.6 %copy-start.5 = (bf16[1,512,1024]{1,2,0:T(8,128)(2,1)S(1)}, bf16[1,512,1024]{1,2,0:T(8,128)(2,1)}, u32[]{:S(2)}) copy-start(bf16[1,512,1024]{1,2,0:T(8,128)(2,1)} %copy.14) | copy-start | bytes 3145732
  51.4 11.6 %copy-start.6 = (bf16[1024,512]{1,0:T(8,128)(2,1)S(1)}, bf16[1024,512]{1,0:T(8,128)(2,1)}, u32[]{:S(2)}) copy-start(bf16[1024,512]{1,0:T(8,128)(2,1)} %convolution_convert_fusion.query_ref) | copy-start | bytes 3145732
  55.7 6.2 %copy-start.14 = (f32[1024,256]{1,0:T(8,128)}, f32[1024,256]{1,0:T(8,128)S(1)}, u32[]{:S(2)}) copy-start(f32[1024,256]{1,0:T(8,128)S(1)} %fusion.16.mine_ref) | copy-start | bytes 3145732
  55.8 6.2 %collective-permute-start.1 = (f32[1024,256]{1,0:T(8,128)S(1)}, f32[1024,256]{1,0:T(8,128)S(1)}, u32[]{:S(2)}, u32[]{:S(2)}) collective-permute-start(f32[1024,256]{1,0:T(8,128)S(1)} %fusion.16.mine_ref), channel_id=1, source_target_pairs={{0,1},{1,0},{2,3},{3,2},{4,5},{5,4},{6,7},{7,6},{8,9},{9,8},{10,11... | collective-permute-start | bytes 3145736 | tf_op jit(solution)/shard_map/ppermute | solution.py:40
  63.0 13.1 %copy-start.13 = (bf16[4,128,512]{2,1,0:T(8,128)(2,1)S(1)}, bf16[4,128,512]{2,1,0:T(8,128)(2,1)}, u32[]{:S(2)}) copy-start(bf16[4,128,512]{2,1,0:T(8,128)(2,1)} %fusion.6) | copy-start | bytes 1572868
  75.7 2.7 %collective-permute-start.2 = (f32[1024,256]{1,0:T(8,128)S(1)}, f32[1024,256]{1,0:T(8,128)S(1)}, u32[]{:S(2)}, u32[]{:S(2)}) collective-permute-start(f32[1024,256]{1,0:T(8,128)S(1)} %get-tuple-element.45), channel_id=1, source_target_pairs={{0,1},{1,0},{2,3},{3,2},{4,5},{5,4},{6,7},{7,6},{8,9},{9,8},{10,11... | collective-permute-start | bytes 3145736 | tf_op jit(solution)/shard_map/ppermute | solution.py:40
  78.3 5.8 %copy-start.17 = (bf16[128,512]{1,0:T(8,128)(2,1)S(1)}, bf16[128,512]{1,0:T(8,128)(2,1)}, u32[]{:S(2)}) copy-start(bf16[128,512]{1,0:T(8,128)(2,1)} %get-tuple-element.51) | copy-start | bytes 393220
  79.5 4.7 %collective-permute-start.3 = (f32[512,1024]{1,0:T(8,128)}, f32[512,1024]{1,0:T(8,128)}, u32[]{:S(2)}, u32[]{:S(2)}) collective-permute-start(f32[512,1024]{1,0:T(8,128)} %fusion.17), channel_id=1, source_target_pairs={{0,1},{1,0},{2,3},{3,2},{4,5},{5,4},{6,7},{7,6},{8,9},{9,8},{10,11... | collective-permute-start | bytes 6291464 | tf_op jit(solution)/shard_map/ppermute | solution.py:40
  79.8 21.9 %all-to-all-start.2 = ((f32[16,64,256]{2,1,0:T(8,128)}), f32[16,64,256]{2,1,0:T(8,128)}, u32[]{:S(2)}, u32[]{:S(2)}) async-start(f32[16,64,256]{2,1,0:T(8,128)} %bitcast.67), calls=%async_computation.2 | async-start | bytes 2097152 | tf_op jit(solution)/shard_map/all_to_all | solution.py:48
  84.2 4.8 %copy-start.16 = (bf16[128,512]{1,0:T(8,128)(2,1)S(1)}, bf16[128,512]{1,0:T(8,128)(2,1)}, u32[]{:S(2)}) copy-start(bf16[128,512]{1,0:T(8,128)(2,1)} %get-tuple-element.52) | copy-start | bytes 393220
  85.6 5.5 %copy-start.15 = (bf16[128,512]{1,0:T(8,128)(2,1)S(1)}, bf16[128,512]{1,0:T(8,128)(2,1)}, u32[]{:S(2)}) copy-start(bf16[128,512]{1,0:T(8,128)(2,1)} %get-tuple-element.49) | copy-start | bytes 393220
  86.5 10.1 %collective-permute-start.5 = (f32[64,1024]{1,0:T(8,128)}, f32[64,1024]{1,0:T(8,128)}, u32[]{:S(2)}, u32[]{:S(2)}) collective-permute-start(f32[64,1024]{1,0:T(8,128)} %get-tuple-element.81), channel_id=1, source_target_pairs={{0,96},{32,0},{64,32},{96,64},{1,97},{33,1},{65,33},{97,65},{2,98}... | collective-permute-start | bytes 786440 | tf_op jit(solution)/shard_map/ppermute | solution.py:44
  88.9 9.0 %collective-permute-start.4 = (f32[64,1024]{1,0:T(8,128)}, f32[64,1024]{1,0:T(8,128)}, u32[]{:S(2)}, u32[]{:S(2)}) collective-permute-start(f32[64,1024]{1,0:T(8,128)} %get-tuple-element.82), channel_id=1, source_target_pairs={{0,32},{32,64},{64,96},{96,0},{1,33},{33,65},{65,97},{97,1},{2,34}... | collective-permute-start | bytes 786440 | tf_op jit(solution)/shard_map/ppermute | solution.py:44
  104.0 20.4 %all-to-all-start.3 = ((f32[16,64,256]{2,1,0:T(8,128)}), f32[16,64,256]{2,1,0:T(8,128)}, u32[]{:S(2)}, u32[]{:S(2)}) async-start(f32[16,64,256]{2,1,0:T(8,128)} %copy-done.2), calls=%async_computation.3 | async-start | bytes 2097152 | tf_op jit(solution)/shard_map/all_to_all | solution.py:48
  108.9 13.3 %collective-permute-start.6 = (f32[128,1024]{1,0:T(8,128)}, f32[128,1024]{1,0:T(8,128)S(1)}, u32[]{:S(2)}, u32[]{:S(2)}) collective-permute-start(f32[128,1024]{1,0:T(8,128)} %get-tuple-element.57), channel_id=1, source_target_pairs={{0,32},{32,64},{64,96},{96,0},{1,33},{33,65},{65,97},{97,1},{2,34}... | collective-permute-start | bytes 1572872 | tf_op jit(solution)/shard_map/ppermute | solution.py:44
  109.6 12.6 %collective-permute-start.7 = (f32[128,1024]{1,0:T(8,128)}, f32[128,1024]{1,0:T(8,128)S(1)}, u32[]{:S(2)}, u32[]{:S(2)}) collective-permute-start(f32[128,1024]{1,0:T(8,128)} %get-tuple-element.58), channel_id=1, source_target_pairs={{0,96},{32,0},{64,32},{96,64},{1,97},{33,1},{65,33},{97,65},{2,98}... | collective-permute-start | bytes 1572872 | tf_op jit(solution)/shard_map/ppermute | solution.py:44
  124.4 19.2 %all-to-all-start.4 = ((f32[16,8,1024]{2,1,0:T(8,128)}), f32[16,8,1024]{2,1,0:T(8,128)}, u32[]{:S(2)}, u32[]{:S(2)}) async-start(f32[16,8,1024]{2,1,0:T(8,128)} %bitcast.70), calls=%async_computation.4 | async-start | bytes 1048576 | tf_op jit(solution)/shard_map/all_to_all | solution.py:48
  133.1 9.7 %collective-permute-start.10 = (f32[16,1024]{1,0:T(8,128)S(1)}, f32[16,1024]{1,0:T(8,128)S(1)}, u32[]{:S(2)}, u32[]{:S(2)}) collective-permute-start(f32[16,1024]{1,0:T(8,128)S(1)} %get-tuple-element.90), channel_id=1, source_target_pairs={{0,96},{32,0},{64,32},{96,64},{1,97},{33,1},{65,33},{97,65},{2,98}... | collective-permute-start | bytes 196616 | tf_op jit(solution)/shard_map/ppermute | solution.py:44
  135.7 7.1 %collective-permute-start.8 = (f32[16,1024]{1,0:T(8,128)S(1)}, f32[16,1024]{1,0:T(8,128)S(1)}, u32[]{:S(2)}, u32[]{:S(2)}) collective-permute-start(f32[16,1024]{1,0:T(8,128)S(1)} %get-tuple-element.89), channel_id=1, source_target_pairs={{0,32},{32,64},{64,96},{96,0},{1,33},{33,65},{65,97},{97,1},{2,34}... | collective-permute-start | bytes 196616 | tf_op jit(solution)/shard_map/ppermute | solution.py:44
  135.7 7.2 %collective-permute-start.9 = (f32[16,1024]{1,0:T(8,128)S(1)}, f32[16,1024]{1,0:T(8,128)S(1)}, u32[]{:S(2)}, u32[]{:S(2)}) collective-permute-start(f32[16,1024]{1,0:T(8,128)S(1)} %get-tuple-element.91), channel_id=1, source_target_pairs={{0,64},{32,96},{64,0},{96,32},{1,65},{33,97},{65,1},{97,33},{2,66}... | collective-permute-start | bytes 196616 | tf_op jit(solution)/shard_map/ppermute | solution.py:44
  142.8 16.6 %copy-start.4 = (f32[1024,256]{1,0:T(8,128)}, f32[1024,256]{1,0:T(8,128)S(1)}, u32[]{:S(2)}) copy-start(f32[1024,256]{1,0:T(8,128)S(1)} %exact_product.1.mine_ref) | copy-start | bytes 3145732
  143.6 15.8 %collective-permute-start.12 = (f32[1024,256]{1,0:T(8,128)S(1)}, f32[1024,256]{1,0:T(8,128)}, u32[]{:S(2)}, u32[]{:S(2)}) collective-permute-start(f32[1024,256]{1,0:T(8,128)S(1)} %exact_product.1.mine_ref), channel_id=1, source_target_pairs={{0,1},{1,0},{2,3},{3,2},{4,5},{5,4},{6,7},{7,6},{8,9},{9,8},{10,11... | collective-permute-start | bytes 3145736 | tf_op jit(solution)/shard_map/ppermute | solution.py:40
  149.2 17.7 %all-to-all-start.5 = ((f32[128,1,128]{2,1,0:T(1,128)}), f32[128,1,128]{2,1,0:T(1,128)S(1)}, u32[]{:S(2)}, u32[]{:S(2)}) async-start(f32[128,1,128]{2,1,0:T(1,128)} %get-tuple-element.64), calls=%async_computation.5 | async-start | bytes 131072 | tf_op jit(solution)/shard_map/all_to_all | solution.py:328
  158.4 5.9 %collective-permute-start.11 = (f32[8,1024]{1,0:T(8,128)S(1)}, f32[8,1024]{1,0:T(8,128)S(1)}, u32[]{:S(2)}, u32[]{:S(2)}) collective-permute-start(f32[8,1024]{1,0:T(8,128)S(1)} %slice_select_fusion), channel_id=1, source_target_pairs={{0,1},{1,0},{2,3},{3,2},{4,5},{5,4},{6,7},{7,6},{8,9},{9,8},{10,11... | collective-permute-start | bytes 98312 | tf_op jit(solution)/shard_map/ppermute | solution.py:40
  (8 other events, 12.3 us)
